TPU v7x, 32 devices: a whole 2x2x4 slice. The times are simulated.
32 devices in a mesh: grp: 2 (over y), gx: 4 (over z), gy: 2 (over x), gz: 2 (over core).
Axes of the slice: x: 2, y: 2, z: 4, core: 2. Of those that a mesh axis runs over, the one named last changes fastest.
Arguments:
- inputs: bfloat16 [2048, 6144], P(('grp', 'gz', 'gy'), 'gx'), parts along dimension 0, may hold values from -6 to 6
- weight: bfloat16 [6144, 24576], P(('gx', 'gz'), 'gy'), may hold values from -0.078125 to 0.078125
- bias: bfloat16 [24576], P('gy'), may hold values from -5 to 5
- cotangent: bfloat16 [2048, 24576], P(('grp', 'gz', 'gx'), 'gy'), parts along dimension 0, may hold values from -0.75 to 0.75
Outputs:
- input_grad: bfloat16 [2048, 6144], P(('grp', 'gz', 'gy'), 'gx'), parts along dimension 0
- weight_grad: bfloat16 [12288, 24576], P(('grp', 'gx', 'gz'), 'gy'), parts along dimension 0
- bias_grad: float32 [49152], P(('grp', 'gy')), parts along dimension 0
There are 2 independent parts, one for each index of `grp`. A program takes and returns all parts, laid end to end along the dimension named above; an argument that names none is the same for every part. Nothing has to cross between parts.
All inputs are finite; a program needn't handle non-finite values.
Results may differ from a plain program's by a relative error of at most 0.011.
Values may be sent and summed in bfloat16 or wider, within the bound.
No kernel may reach another device: no remote copies, remote signals or barrier semaphores. Data moves between devices by JAX's collectives and lax.ppermute only.
A program may use at most 256 MiB of HBM per device.

v0:
```python
import jax
import jax.numpy as jnp
from jax import lax
from jax.sharding import PartitionSpec as P


def gelu_slope(preact):
    scale = 0.7978845608028654
    inner = scale * (preact + 0.044715 * preact * preact * preact)
    bend = jnp.tanh(inner)
    return 0.5 * (1.0 + bend) + 0.5 * preact * (1.0 - bend * bend) * scale * (
        1.0 + 3.0 * 0.044715 * preact * preact
    )


def shards(inputs, weight, bias, cotangent):
    token_rows = lax.all_gather(inputs, "gy", axis=0, tiled=True)
    weight_block = lax.all_gather(weight, "gz", axis=0, tiled=True)
    partial_value = jnp.dot(token_rows, weight_block, preferred_element_type=jnp.float32)
    bias_value = bias.astype(jnp.float32)
    preact = lax.psum(partial_value.astype(jnp.bfloat16), "gx").astype(jnp.float32) + bias_value
    grad_rows = lax.all_gather(cotangent, "gx", axis=0, tiled=True)
    pre_grad = (grad_rows.astype(jnp.float32) * gelu_slope(preact)).astype(jnp.bfloat16)
    bias_grad = lax.psum(jnp.sum(pre_grad, axis=0, dtype=jnp.float32), "gz")
    input_grad = lax.psum_scatter(
        lax.dot_general(
            pre_grad, weight_block, (((1,), (1,)), ((), ())), preferred_element_type=jnp.float32
        ).astype(jnp.bfloat16),
        "gy",
        scatter_dimension=0,
        tiled=True,
    )
    weight_grad = lax.psum_scatter(
        lax.dot_general(
            token_rows, pre_grad, (((0,), (0,)), ((), ())), preferred_element_type=jnp.float32
        ).astype(jnp.bfloat16),
        "gz",
        scatter_dimension=0,
        tiled=True,
    )
    return (input_grad, weight_grad, bias_grad)


def solution(mesh):
    placed = (
        P(("grp", "gz", "gy"), "gx"),
        P(("gx", "gz"), "gy"),
        P("gy"),
        P(("grp", "gz", "gx"), "gy"),
    )
    return jax.shard_map(
        shards,
        mesh=mesh,
        in_specs=placed,
        out_specs=(P(("grp", "gz", "gy"), "gx"), P(("grp", "gx", "gz"), "gy"), P(("grp", "gy"))),
        check_vma=False,
    )
```

profile of v0, /device:TPU:0, one launch (start us, length us, event | category | flops | bytes accessed | tf_op | source)
XLA Modules:
  0.0 883.8 jit_solution(2385431500357307470)
XLA Ops:
  7.2 0.0 all-gather.6.cloned.1.call-start
  7.2 0.7 all-gather.6.cloned.1.call-update
  7.9 0.0 all-gather.8.cloned.1.call-start
  7.9 0.7 all-gather.8.cloned.1.call-update
  8.6 0.0 all-gather.4.cloned.1.call-start
  8.7 0.7 all-gather.4.cloned.1.call-update
  9.4 0.0 copy-start
  9.4 0.0 all-reduce.2.cloned.1.call-start
  9.4 30.0 %all-gather.6.cloned.1.call-done = bf16[512,1536]{1,0:T(8,128)(2,1)} async-done(((bf16[256,1536]{1,0:T(8,128)(2,1)}), bf16[512,1536]{1,0:T(8,128)(2,1)}) %all-gather.6.cloned.1.call-update) | async-done | bytes 1572880 | tf_op jit(solution)/shard_map/all_gather | solution.py:17
  39.5 59.4 %all-gather.8.cloned.1.call-done = bf16[1536,12288]{1,0:T(8,128)(2,1)} async-done(((bf16[768,12288]{1,0:T(8,128)(2,1)}), bf16[1536,12288]{1,0:T(8,128)(2,1)}) %all-gather.8.cloned.1.call-update) | async-done | bytes 37748752 | tf_op jit(solution)/shard_map/all_gather | solution.py:18
  98.9 27.5 %convolution_convert_fusion.1 = bf16[512,12288]{1,0:T(8,128)(2,1)} fusion(bf16[512,1536]{1,0:T(8,128)(2,1)} %all-gather.6.cloned.1.call-done, bf16[1536,12288]{1,0:T(8,128)(2,1)} %all-gather.8.cloned.1.call-done), kind=kOutput, calls=%fused_computation.12 | convolution fusion | flops 19333644288 | bytes 51904512 | tf_op jit(solution)/shard_map/dot_general | solution.py:19
  126.4 0.0 copy-start.1
  126.4 0.0 all-reduce.2.cloned.1.call-update
  126.4 0.2 reduce-scatter.5.cloned.1.call-start
  126.7 0.0 copy-done
  126.7 193.2 %all-gather.4.cloned.1.call-done = bf16[512,12288]{1,0:T(8,128)(2,1)} async-done(((bf16[128,12288]{1,0:T(8,128)(2,1)}), bf16[512,12288]{1,0:T(8,128)(2,1)}) %all-gather.4.cloned.1.call-update) | async-done | bytes 12582928 | tf_op jit(solution)/shard_map/all_gather | solution.py:22
  319.9 427.2 %all-reduce.2.cloned.1.call-done = bf16[512,12288]{1,0:T(8,128)(2,1)} async-done(((bf16[512,12288]{1,0:T(8,128)(2,1)}), bf16[512,12288]{1,0:T(8,128)(2,1)}) %all-reduce.2.cloned.1.call-update) | async-done | bytes 12582928 | tf_op jit(solution)/shard_map/psum | solution.py:21
  747.1 22.9 %convert_reduce_fusion = (f32[12288]{0:T(1024)S(1)}, bf16[512,12288]{1,0:T(8,128)(2,1)}) fusion(f32[12288]{0:T(1024)S(1)} %convert_element_type.30, bf16[512,12288]{1,0:T(8,128)(2,1)} %all-reduce.2.cloned.1.call-done, bf16[512,12288]{1,0:T(8,128)(2,1)} %all-gather.4.cloned.1.call-done), kind=kLoop, calls=%fused_computation.11 | loop fusion | flops 150982656 | bytes 37847040 | tf_op jit(solution)/shard_map/reduce_sum | solution.py:24
  770.0 0.0 copy-done.1
  770.0 28.5 %fusion = bf16[1536,12288]{0,1:T(8,128)(2,1)} fusion(bf16[512,12288]{1,0:T(8,128)(2,1)} %get-tuple-element.7, bf16[512,1536]{1,0:T(8,128)(2,1)S(1)} %copy-done.1), kind=kOutput, calls=%fused_computation.1 | convolution fusion | flops 19346227200 | bytes 51904512 | tf_op jit(solution)/shard_map/dot_general | solution.py:34
  798.5 0.0 reduce-scatter.5.cloned.1.call-update
  798.5 0.0 reduce-scatter.3.cloned.1.call-start
  798.6 30.5 %convolution_convert_fusion.2 = bf16[512,1536]{1,0:T(8,128)(2,1)} fusion(bf16[512,12288]{1,0:T(8,128)(2,1)} %get-tuple-element.7, bf16[1536,12288]{1,0:T(8,128)(2,1)} %all-gather.8.cloned.1.call-done), kind=kOutput, calls=%fused_computation.13 | convolution fusion | flops 19328139264 | bytes 51904512 | tf_op jit(solution)/shard_map/dot_general | solution.py:26
  829.1 0.0 reduce-scatter.3.cloned.1.call-update
  829.1 4.1 psum.15
  833.2 13.6 %reduce-scatter.5.cloned.1.call-done = bf16[768,12288]{0,1:T(8,128)(2,1)} async-done(((bf16[1536,12288]{0,1:T(8,128)(2,1)}), bf16[768,12288]{0,1:T(8,128)(2,1)}) %reduce-scatter.5.cloned.1.call-update) | async-done | bytes 18874384 | tf_op jit(solution)/shard_map/reduce_scatter | solution.py:33
  846.8 24.6 %copy.7 = bf16[768,12288]{1,0:T(8,128)(2,1)} copy(bf16[768,12288]{0,1:T(8,128)(2,1)} %reduce-scatter.5.cloned.1.call-done) | data formatting | bytes 37748736
  871.5 5.5 reduce-scatter.3.cloned.1.call-done
  (1 shorter events, 0.0 us)
Async XLA Ops:
  7.2 32.3 %all-gather.6.cloned.1.call-start = ((), (), s32[]{:S(2)}) async-start(), calls=%async_computation.3 | async-start | bytes 2359296 | tf_op jit(solution)/shard_map/all_gather | solution.py:17
  7.9 91.0 %all-gather.8.cloned.1.call-start = ((), (), s32[]{:S(2)}) async-start(), calls=%async_computation.4 | async-start | bytes 56623104 | tf_op jit(solution)/shard_map/all_gather | solution.py:18
  8.6 311.2 %all-gather.4.cloned.1.call-start = ((), (), s32[]{:S(2)}) async-start(), calls=%async_computation.2 | async-start | bytes 15728640 | tf_op jit(solution)/shard_map/all_gather | solution.py:22
  9.4 117.3 %copy-start = (bf16[12288]{0:T(1024)(128)(2,1)S(1)}, bf16[12288]{0:T(1024)(128)(2,1)}, u32[]{:S(2)}) copy-start(bf16[12288]{0:T(1024)(128)(2,1)} %param.6) | copy-start | bytes 73732
  9.4 737.7 %all-reduce.2.cloned.1.call-start = ((), (), s32[]{:S(2)}) async-start(), calls=%async_computation.5 | async-start | bytes 25165824 | tf_op jit(solution)/shard_map/psum | solution.py:21
  126.4 643.5 %copy-start.1 = (bf16[512,1536]{1,0:T(8,128)(2,1)S(1)}, bf16[512,1536]{1,0:T(8,128)(2,1)}, u32[]{:S(2)}) copy-start(bf16[512,1536]{1,0:T(8,128)(2,1)} %all-gather.6.cloned.1.call-done) | copy-start | bytes 4718596
  126.4 720.4 %reduce-scatter.5.cloned.1.call-start = ((), (), s32[]{:S(2)}) async-start(), calls=%async_computation.7 | async-start | bytes 56623104 | tf_op jit(solution)/shard_map/reduce_scatter | solution.py:33
  798.5 78.4 %reduce-scatter.3.cloned.1.call-start = ((), (), s32[]{:S(2)}) async-start(), calls=%async_computation.6 | async-start | bytes 2359296 | tf_op jit(solution)/shard_map/reduce_scatter | solution.py:25
Sparse Core Ops, SparseCore 0:
  9.5 29.8 all-gather.5
  41.0 57.7 all-gather.7
  100.5 219.3 all-gather.3
  322.8 424.2 all-reduce.1
  798.7 48.1 reduce-scatter.4
  849.5 27.3 reduce-scatter.2
where the time goes:
time: 885 us; the launch traced here: 884 us
  waiting for transfers between devices  731 us (83%)
  matrix products  86.6 us (10%)
  local copies, waits for them, and re-layouts  24.6 us (3%)
  other arithmetic  22.9 us (3%)
  between operations  14.1 us (2%)
    psum x1, waiting for transfers between devices, shards(): lax.psum(partial_value.astype(jnp.bfloat16), 'gx').astype(jnp.float32)  427 us
    all_gather x1, waiting for transfers between devices, shards(): grad_rows = lax.all_gather(cotangent, 'gx', axis=0, tiled=True)  193 us
    all_gather x1, waiting for transfers between devices, shards(): weight_block = lax.all_gather(weight, 'gz', axis=0, tiled=True)  59.4 us
    dot_general x1, matrix products, shards(): lax.dot_general(pre_grad, weight_block, (((1,), (1,)), ((), ())), preferr...  30.5 us
    all_gather x1, waiting for transfers between devices, shards(): token_rows = lax.all_gather(inputs, 'gy', axis=0, tiled=True)  30 us
    dot_general x1, matrix products, shards(): lax.dot_general(token_rows, pre_grad, (((0,), (0,)), ((), ())), preferred...  28.5 us
    dot_general x1, matrix products, shards(): jnp.dot(token_rows, weight_block, preferred_element_type=jnp.float32)  27.5 us
    unnamed x5, local copies, waits for them, and re-layouts  24.6 us
  transfers between devices with their start and end apart: 6, of which 6 were waited for; matrix products, arithmetic and copies ran while one was open for 9% of the time, Pallas kernels for 0%

commit v1 on v0

v1 whole, which is shorter than its diff:
```python
import functools

import jax
import jax.numpy as jnp
from jax import lax
from jax.sharding import PartitionSpec as P

F32, BF16 = jnp.float32, jnp.bfloat16


def gelu_slope(preact):
    scale = 0.7978845608028654
    inner = scale * (preact + 0.044715 * preact * preact * preact)
    bend = jnp.tanh(inner)
    return 0.5 * (1.0 + bend) + 0.5 * preact * (1.0 - bend * bend) * scale * (
        1.0 + 3.0 * 0.044715 * preact * preact
    )


def by_core(core, first, second):
    return jnp.where(core == 0, first, second)


def swap(value, axis):
    return lax.ppermute(value, axis, [(0, 1), (1, 0)])


def gather_tokens(inputs, nx, ny, core):
    rows, features = inputs.shape
    if ny == 2:
        side = lax.axis_index("gy")
        beside = swap(inputs, "gy")
        other = swap(inputs, "gz")
        other_beside = swap(beside, "gz")
        mine = jnp.concatenate([by_core(side, inputs, beside), by_core(side, beside, inputs)])
        theirs = jnp.concatenate([by_core(side, other, other_beside), by_core(side, other_beside, other)])
    else:
        mine = lax.all_gather(inputs, "gy", axis=0, tiled=True)
        theirs = swap(mine, "gz")
    both = jnp.stack([by_core(core, mine, theirs), by_core(core, theirs, mine)])
    both = both.reshape(2, nx, rows * ny // nx, features).transpose(1, 0, 2, 3)
    return both.reshape(2 * rows * ny, features)


def pieces(half, nx):
    count = 8 if nx <= 4 else 2
    width = half // count
    return [(c * width, width) for c in range(count)]


def after(value, *others):
    return lax.optimization_barrier((value, *others))[0] if others else value


class Line:
    def __init__(self, n, rank, block):
        self.n, self.rank, self.block = n, rank, block

    def first(self, partial):
        n, rank, block = self.n, self.rank, self.block
        self.partial, self.width = partial, partial.shape[1]
        self.received, self.sums = None, []
        return self.reduce_send(0)

    def reduce_send(self, s):
        n, rank, block = self.n, self.rank, self.block
        size = (n - 1 - s) * block
        start = jnp.where(rank == s, (s + 1) * block, 0)
        send = lax.dynamic_slice(self.partial, (start, 0), (size, self.width))
        if s > 0:
            came = lax.dynamic_slice(self.received, (jnp.where(rank == s, block, 0), 0), (size, self.width))
            send = (send.astype(F32) + came.astype(F32)).astype(BF16)
        return send

    def reduce_permute(self, s, send):
        n = self.n
        self.received = lax.ppermute(send, "gx", [(s, s + 1), (n - 1 - s, n - 2 - s)])
        self.sums.append(self.received)

    def reduced(self):
        n, rank, block = self.n, self.rank, self.block
        own = lax.dynamic_slice(self.partial, (rank * block, 0), (block, self.width)).astype(F32)
        for s, received in enumerate(self.sums):
            size = (n - 1 - s) * block
            own = own + jnp.where(rank == s + 1, received[:block], 0).astype(F32)
            own = own + jnp.where(rank == n - 2 - s, received[size - block :], 0).astype(F32)
        return own

    def gather_first(self, own):
        n, rank, block = self.n, self.rank, self.block
        whole = jnp.zeros((n * block, self.width), own.dtype)
        self.whole = lax.dynamic_update_slice(whole, own, (rank * block, 0))
        return own

    def gather_send(self, u):
        n, rank, block = self.n, self.rank, self.block
        size = (u + 1) * block
        return lax.dynamic_slice(
            self.whole, (jnp.where(rank == u, 0, (n - 1 - u) * block), 0), (size, self.width)
        )

    def gather_permute(self, u, send):
        n = self.n
        self.received = lax.ppermute(send, "gx", [(u, u + 1), (n - 1 - u, n - 2 - u)])

    def gather_place(self, u):
        n, rank, block = self.n, self.rank, self.block
        size = (u + 1) * block
        start = jnp.where(rank == u + 1, 0, (n - 1 - u) * block)
        takes = (rank == u + 1) | (rank == n - 2 - u)
        kept = lax.dynamic_slice(self.whole, (start, 0), (size, self.width))
        whole = jnp.where(takes, self.received, kept)
        self.whole = lax.dynamic_update_slice(self.whole, whole, (start, 0))


def shards(inputs, weight, bias, cotangent, *, nx, ny):
    core, rank = lax.axis_index("gz"), lax.axis_index("gx")
    rows, features = inputs.shape
    mine, hidden = weight.shape
    half = hidden // 2
    block = 2 * rows * ny // nx

    def halves(value, start, width):
        left, right = value[..., start : start + width], value[..., half + start : half + start + width]
        return by_core(core, left, right), by_core(core, right, left)

    tokens = gather_tokens(inputs, nx, ny, core)
    tokens = jnp.concatenate(
        [
            by_core(core, tokens[:, :mine], tokens[:, mine:]),
            by_core(core, tokens[:, mine:], tokens[:, :mine]),
        ],
        axis=1,
    )
    cot_own, cot_send = halves(cotangent, 0, half)
    cot_other = swap(cot_send, "gz")
    cot = jnp.concatenate([by_core(core, cot_own, cot_other), by_core(core, cot_other, cot_own)])
    bias_own, _ = halves(bias, 0, half)
    bias_own = bias_own.astype(F32)

    weight_grad = jnp.zeros((mine, hidden), BF16)
    input_sum = jnp.zeros((tokens.shape[0], features), F32)
    chunks = pieces(half, nx)
    count, steps = len(chunks), nx - 1
    lines = [Line(nx, rank, block) for _ in chunks]
    bias_sums, weights, sends = [], {}, {}
    last = []

    def ordered(value):
        return after(value, *last)

    def note(*values):
        last[:] = values

    def multiply(c):
        start, width = chunks[c]
        w_own, w_send = halves(weight, start, width)
        w = jnp.concatenate([w_own, swap(w_send, "gz")])
        weights[c] = w
        partial = jnp.dot(tokens, ordered(w), preferred_element_type=F32).astype(BF16)
        sends[c] = lines[c].first(partial)
        note(sends[c])

    def reduce_start(c):
        lines[c].reduce_permute(0, ordered(sends[c]))

    def reduce_next(c, s):
        lines[c].received = ordered(lines[c].received)
        send = lines[c].reduce_send(s)
        note(send)
        lines[c].reduce_permute(s, send)

    def slope(c):
        start, width = chunks[c]
        lines[c].sums[-1] = ordered(lines[c].sums[-1])
        preact = lines[c].reduced() + bias_own[start : start + width]
        grad = (cot[:, start : start + width].astype(F32) * gelu_slope(preact)).astype(BF16)
        note(grad)
        lines[c].gather_permute(0, lines[c].gather_first(grad))

    def gather_next(c, u):
        lines[c].received = ordered(lines[c].received)
        lines[c].gather_place(u - 1)
        send = lines[c].gather_send(u)
        note(send)
        lines[c].gather_permute(u, send)

    def use(c):
        nonlocal weight_grad, input_sum
        start, width = chunks[c]
        lines[c].received = ordered(lines[c].received)
        lines[c].gather_place(steps - 1)
        grad = lines[c].whole
        bias_sums.append(jnp.sum(grad, axis=0, dtype=F32))
        w_grad = lax.dot_general(tokens, grad, (((0,), (0,)), ((), ())), preferred_element_type=F32).astype(BF16)
        w_own, w_other = w_grad[:mine], swap(w_grad[mine:], "gz")
        input_sum = input_sum + lax.dot_general(
            grad, weights[c], (((1,), (1,)), ((), ())), preferred_element_type=F32
        )
        note(w_grad, input_sum)
        weight_grad = weight_grad.at[:, start : start + width].set(by_core(core, w_own, w_other))
        weight_grad = weight_grad.at[:, half + start : half + start + width].set(by_core(core, w_other, w_own))

    def do(step, c, *rest):
        if 0 <= c < count:
            step(c, *rest)

    if nx == 4:
        do(multiply, 0)
        for i in range(count + 4):
            do(reduce_start, i)
            do(gather_next, i - 2, 1)
            do(reduce_next, i - 1, 2)
            do(multiply, i + 1)
            do(use, i - 4)
            do(slope, i - 1)
            do(gather_next, i - 2, 2)
            do(reduce_next, i, 1)
    else:
        for c in range(count):
            multiply(c)
            reduce_start(c)
            for s in range(1, steps):
                reduce_next(c, s)
            slope(c)
            for u in range(1, steps):
                gather_next(c, u)
            use(c)

    bias_own = jnp.concatenate(bias_sums)
    bias_other = swap(bias_own, "gz")
    bias_grad = jnp.concatenate([by_core(core, bias_own, bias_other), by_core(core, bias_other, bias_own)])

    input_sum = jnp.concatenate(
        [
            by_core(core, input_sum[:, :mine], input_sum[:, mine:]),
            by_core(core, input_sum[:, mine:], input_sum[:, :mine]),
        ],
        axis=1,
    )
    by_token = input_sum.reshape(nx, 2, block // 2, features)
    kept = by_core(core, by_token[:, 0], by_token[:, 1]).reshape(rows * ny, features)
    sent = by_core(core, by_token[:, 1], by_token[:, 0]).reshape(rows * ny, features)
    term = kept + swap(sent.astype(BF16), "gz").astype(F32)
    if ny == 2:
        side = lax.axis_index("gy")
        kept = by_core(side, term[:rows], term[rows:])
        sent = by_core(side, term[rows:], term[:rows])
        input_grad = (kept + swap(sent.astype(BF16), "gy").astype(F32)).astype(BF16)
    else:
        input_grad = lax.psum_scatter(term.astype(BF16), "gy", scatter_dimension=0, tiled=True)
    return input_grad, weight_grad, bias_grad


def solution(mesh):
    placed = (
        P(("grp", "gz", "gy"), "gx"),
        P(("gx", "gz"), "gy"),
        P("gy"),
        P(("grp", "gz", "gx"), "gy"),
    )
    return jax.shard_map(
        functools.partial(shards, nx=mesh.shape["gx"], ny=mesh.shape["gy"]),
        mesh=mesh,
        in_specs=placed,
        out_specs=(P(("grp", "gz", "gy"), "gx"), P(("grp", "gx", "gz"), "gy"), P(("grp", "gy"))),
        check_vma=False,
    )
```

time: 885 us -> 575 us (0.65)
  waiting for transfers between devices: 731 us -> 150 us
  starting transfers between devices: 0.42 us -> 139 us
  other arithmetic: 22.9 us -> 123 us
  matrix products: 86.6 us -> 107 us
  local copies, waits for them, and re-layouts: 24.6 us -> 44.3 us
  between operations: 14.1 us -> 2.94 us
    psum x1 -> x0, waiting for transfers between devices: 427 us -> none  [shards(): lax.psum(partial_value.astype(jnp.bfloat16), 'gx').astype(jnp.float32)]
    all_gather x3 -> x0, waiting for transfers between devices: 283 us -> none  [the longest x1 193 us: shards(): grad_rows = lax.all_gather(cotangent, 'gx', axis=0, tiled=True)]
    ppermute x0 -> x71, waiting for transfers between devices: none -> 150 us  [the longest x24 84.9 us: reduce_permute(): lax.ppermute(send, 'gx', [(s, s + 1), (n - 1 - s, n - 2 - s)])]
    ppermute x0 -> x71, starting transfers between devices: none -> 139 us  [the longest x24 67.7 us: reduce_permute(): lax.ppermute(send, 'gx', [(s, s + 1), (n - 1 - s, n - 2 - s)])]
    dynamic_update_slice x0 -> x32, other arithmetic: none -> 36.3 us  [the longest x24 21.4 us: gather_place(): self.whole = lax.dynamic_update_slice(self.whole, whole, (start, 0))]
    scatter x0 -> x15, other arithmetic: none -> 25.8 us  [the longest x8 17.2 us: use(): weight_grad.at[:, half + start:half + start + width]]
    select_n x0 -> x9, other arithmetic: none -> 20.4 us  [by_core(): return jnp.where(core == 0, first, second)]
    dot_general x3 -> x24, matrix products: 86.6 us -> 107 us  [the longest x8 55 us: use(): lax.dot_general(grad, weights[c], (((1,), (1,)), ((), ())), preferred_ele...]
  transfers between devices with their start and end apart: 6 -> 71, of which waited for: 6 -> 19; matrix products, arithmetic and copies ran while one was open for 9% -> 46% of each run, Pallas kernels for 0% -> 0%
where the time goes in v1:
time: 575 us; the launch traced here: 566 us
  waiting for transfers between devices  150 us (26%)
  starting transfers between devices  139 us (24%)
  other arithmetic  123 us (21%)
  matrix products  107 us (19%)
  local copies, waits for them, and re-layouts  44.3 us (8%)
    ppermute x24, waiting for transfers between devices, reduce_permute(): lax.ppermute(send, 'gx', [(s, s + 1), (n - 1 - s, n - 2 - s)])  84.9 us
    ppermute x24, starting transfers between devices, reduce_permute(): lax.ppermute(send, 'gx', [(s, s + 1), (n - 1 - s, n - 2 - s)])  67.7 us
    ppermute x24, starting transfers between devices, gather_permute(): lax.ppermute(send, 'gx', [(u, u + 1), (n - 1 - u, n - 2 - u)])  62.8 us
    dot_general x8, matrix products, use(): lax.dot_general(grad, weights[c], (((1,), (1,)), ((), ())), preferred_ele...  55 us
    ppermute x24, waiting for transfers between devices, gather_permute(): lax.ppermute(send, 'gx', [(u, u + 1), (n - 1 - u, n - 2 - u)])  50.8 us
    dot_general x8, matrix products, use(): lax.dot_general(tokens, grad, (((0,), (0,)), ((), ())), preferred_element...  27.1 us
    dot_general x8, matrix products, multiply(): jnp.dot(tokens, ordered(w), preferred_element_type=F32).astype(BF16)  24.4 us
    dynamic_update_slice x24, other arithmetic, gather_place(): self.whole = lax.dynamic_update_slice(self.whole, whole, (start, 0))  21.4 us
  transfers between devices with their start and end apart: 71, of which 19 were waited for; matrix products, arithmetic and copies ran while one was open for 46% of the time, Pallas kernels for 0%

profile of v1, /device:TPU:0, one launch (start us, length us, event | category | flops | bytes accessed | tf_op | source)
XLA Modules:
  0.0 566.2 jit_solution(11541755488968541533)
XLA Ops:
  3.6 3.3 broadcast_select_fusion.4
  7.5 7.4 %broadcast_select_fusion.8 = (bf16[768,768]{1,0:T(8,128)(2,1)}, bf16[768,768]{1,0:T(8,128)(2,1)}, bf16[768,768]{1,0:T(8,128)(2,1)}, bf16[768,768]{1,0:T(8,128)(2...) fusion(pred[]{:T(512)S(6)} %eq.13, bf16[768,12288]{1,0:T(8,128)(2,1)} %param.37), kind=kLoop, calls=%fused_computation.135 | loop fusion | flops 4128768 | bytes 17694720 | tf_op jit(solution)/shard_map/jit(_where)/select_n | solution.py:21
  17.3 3.4 broadcast_select_fusion.9
  28.4 4.7 convolution_convert_fusion.15
  33.3 3.8 collective-permute-start.5
  42.3 20.6 %collective-permute-done.5 = bf16[768,768]{1,0:T(8,128)(2,1)S(1)} collective-permute-done((bf16[768,768]{1,0:T(8,128)(2,1)S(1)}, bf16[768,768]{1,0:T(8,128)(2,1)S(1)}, u32[]{:S(2)}, u32[]{:S(2)}) %collective-permute-start.5) | collective-permute-done | bytes 1179680 | tf_op jit(solution)/shard_map/ppermute | solution.py:77
  65.5 7.2 %collective-permute-start.11 = (bf16[768,768]{1,0:T(8,128)(2,1)S(1)}, bf16[768,768]{1,0:T(8,128)(2,1)S(1)}, u32[]{:S(2)}, u32[]{:S(2)}) collective-permute-start(bf16[768,768]{1,0:T(8,128)(2,1)S(1)} %constant_dynamic-slice_fusion.22), channel_id=1, source_target_pairs={{0,4},{12,8},{1,5},{13,9},{2,6},{14,10},{3,7},{15,11},{16,20},{28,... | collective-permute-start | bytes 3538952 | tf_op jit(solution)/shard_map/ppermute | solution.py:77
  78.3 17.7 %collective-permute-done.8 = bf16[256,768]{1,0:T(8,128)(2,1)S(1)} collective-permute-done((bf16[256,768]{1,0:T(8,128)(2,1)S(1)}, bf16[256,768]{1,0:T(8,128)(2,1)S(1)}, u32[]{:S(2)}, u32[]{:S(2)}) %collective-permute-start.8) | collective-permute-done | bytes 393248 | tf_op jit(solution)/shard_map/ppermute | solution.py:77
  102.1 3.4 collective-permute-start.10
  128.9 8.9 %collective-permute-done.14 = bf16[256,768]{1,0:T(8,128)(2,1)S(1)} collective-permute-done((bf16[256,768]{1,0:T(8,128)(2,1)S(1)}, bf16[256,768]{1,0:T(8,128)(2,1)S(1)}, u32[]{:S(2)}, u32[]{:S(2)}) %collective-permute-start.14) | collective-permute-done | bytes 393248 | tf_op jit(solution)/shard_map/ppermute | solution.py:77
  145.5 4.4 collective-permute-start.20
  153.5 4.0 collective-permute-start.19
  160.4 11.7 %collective-permute-start.23 = (bf16[256,768]{1,0:T(8,128)(2,1)S(1)}, bf16[256,768]{1,0:T(8,128)(2,1)S(1)}, u32[]{:S(2)}, u32[]{:S(2)}) collective-permute-start(bf16[256,768]{1,0:T(8,128)(2,1)S(1)} %add_convert_fusion.14), channel_id=1, source_target_pairs={{8,12},{4,0},{9,13},{5,1},{10,14},{6,2},{11,15},{7,3},{24,28},{20,... | collective-permute-start | bytes 1179656 | tf_op jit(solution)/shard_map/ppermute | solution.py:77
  174.8 6.2 %collective-permute-done.23 = bf16[256,768]{1,0:T(8,128)(2,1)S(1)} collective-permute-done((bf16[256,768]{1,0:T(8,128)(2,1)S(1)}, bf16[256,768]{1,0:T(8,128)(2,1)S(1)}, u32[]{:S(2)}, u32[]{:S(2)}) %collective-permute-start.23) | collective-permute-done | bytes 393248 | tf_op jit(solution)/shard_map/ppermute | solution.py:77
  182.2 7.3 %collective-permute-start.26 = (bf16[256,768]{1,0:T(8,128)(2,1)S(1)}, bf16[256,768]{1,0:T(8,128)(2,1)S(1)}, u32[]{:S(2)}, u32[]{:S(2)}) collective-permute-start(bf16[256,768]{1,0:T(8,128)(2,1)S(1)} %get-tuple-element.332), channel_id=1, source_target_pairs={{0,4},{12,8},{1,5},{13,9},{2,6},{14,10},{3,7},{15,11},{16,20},{28,... | collective-permute-start | bytes 1179656 | tf_op jit(solution)/shard_map/ppermute | solution.py:104
  199.0 5.7 %collective-permute-start.29 = (bf16[768,768]{1,0:T(8,128)(2,1)S(1)}, bf16[768,768]{1,0:T(8,128)(2,1)S(1)}, u32[]{:S(2)}, u32[]{:S(2)}) collective-permute-start(bf16[768,768]{1,0:T(8,128)(2,1)S(1)} %constant_dynamic-slice_fusion.13), channel_id=1, source_target_pairs={{0,4},{12,8},{1,5},{13,9},{2,6},{14,10},{3,7},{15,11},{16,20},{28,... | collective-permute-start | bytes 3538952 | tf_op jit(solution)/shard_map/ppermute | solution.py:77
  210.7 16.4 %collective-permute-done.16 = bf16[768,768]{1,0:T(8,128)(2,1)S(1)} collective-permute-done((bf16[768,768]{1,0:T(8,128)(2,1)S(1)}, bf16[768,768]{1,0:T(8,128)(2,1)S(1)}, u32[]{:S(2)}, u32[]{:S(2)}) %collective-permute-start.16) | collective-permute-done | bytes 1179680 | tf_op jit(solution)/shard_map/ppermute | solution.py:104
  231.5 4.7 convolution_convert_fusion.7
  237.5 7.1 %fusion = f32[1024,1536]{1,0:T(8,128)} fusion(bf16[1024,768]{1,0:T(8,128)(2,1)} %select_dynamic-update-slice_fusion.9, bf16[768,768]{1,0:T(8,128)(2,1)} %collective-permute-done.4, bf16[768,768]{1,0:T(8,128)(2,1)S(1)} %copy-done.45), kind=kOutput, calls=%fused_computation.81 | convolution fusion | flops 2420637696 | bytes 10223616 | tf_op jit(solution)/shard_map/dot_general | solution.py:197
  244.5 13.6 %collective-permute-done.31 = bf16[256,768]{1,0:T(8,128)(2,1)S(1)} collective-permute-done((bf16[256,768]{1,0:T(8,128)(2,1)S(1)}, bf16[256,768]{1,0:T(8,128)(2,1)S(1)}, u32[]{:S(2)}, u32[]{:S(2)}) %collective-permute-start.31) | collective-permute-done | bytes 393248 | tf_op jit(solution)/shard_map/ppermute | solution.py:77
  266.8 5.4 collective-permute-start.36
  280.9 4.0 convolution_convert_fusion.9
  292.7 7.1 %convolution_add_fusion.6 = f32[1024,1536]{1,0:T(8,128)} fusion(f32[1024,1536]{1,0:T(8,128)} %fusion, bf16[1024,768]{1,0:T(8,128)(2,1)S(1)} %select_dynamic-update-slice_fusion.8, bf16[768,768]{1,0:T(8,128)(2,1)} %collective-permute-done.6, bf16[768,768]{1,0:T(8,128)(2,1)} %copy-done.22), kind=kOutput, calls=%fused_computation.21 | convolution fusion | flops 2422210560 | bytes 16515072 | tf_op jit(solution)/shard_map/dot_general | solution.py:197
  303.0 7.2 %collective-permute-start.40 = (bf16[256,768]{1,0:T(8,128)(2,1)S(1)}, bf16[256,768]{1,0:T(8,128)(2,1)S(1)}, u32[]{:S(2)}, u32[]{:S(2)}) collective-permute-start(bf16[256,768]{1,0:T(8,128)(2,1)S(1)} %get-tuple-element.328), channel_id=1, source_target_pairs={{0,4},{12,8},{1,5},{13,9},{2,6},{14,10},{3,7},{15,11},{16,20},{28,... | collective-permute-start | bytes 1179656 | tf_op jit(solution)/shard_map/ppermute | solution.py:104
  315.1 4.2 collective-permute-done.40
  319.3 5.5 collective-permute-start.42
  339.1 3.2 convolution_convert_fusion.5
  343.4 7.1 %convolution_add_fusion.5 = f32[1024,1536]{1,0:T(8,128)} fusion(f32[1024,1536]{1,0:T(8,128)} %convolution_add_fusion.6, bf16[1024,768]{1,0:T(8,128)(2,1)S(1)} %select_dynamic-update-slice_fusion.7, bf16[768,768]{1,0:T(8,128)(2,1)} %copy-done.52, bf16[768,768]{1,0:T(8,128)(2,1)} %copy-done.21), kind=kOutput, calls=%fused_computation.20 | convolution fusion | flops 2422210560 | bytes 16515072 | tf_op jit(solution)/shard_map/dot_general | solution.py:197
  353.2 9.9 %collective-permute-start.46 = (bf16[256,768]{1,0:T(8,128)(2,1)S(1)}, bf16[256,768]{1,0:T(8,128)(2,1)S(1)}, u32[]{:S(2)}, u32[]{:S(2)}) collective-permute-start(bf16[256,768]{1,0:T(8,128)(2,1)S(1)} %get-tuple-element.326), channel_id=1, source_target_pairs={{0,4},{12,8},{1,5},{13,9},{2,6},{14,10},{3,7},{15,11},{16,20},{28,... | collective-permute-start | bytes 1179656 | tf_op jit(solution)/shard_map/ppermute | solution.py:104
  368.6 3.5 collective-permute-done.46
  372.1 5.4 collective-permute-start.48
  387.5 3.3 convolution_convert_fusion.4
  391.9 7.1 %convolution_add_fusion.4 = f32[1024,1536]{1,0:T(8,128)} fusion(f32[1024,1536]{1,0:T(8,128)} %convolution_add_fusion.5, bf16[1024,768]{1,0:T(8,128)(2,1)S(1)} %select_dynamic-update-slice_fusion.6, bf16[768,768]{1,0:T(8,128)(2,1)} %collective-permute-done.15, bf16[768,768]{1,0:T(8,128)(2,1)} %get-tuple-element.342), kind=kOutput, calls=%fused_computation.19 | convolution fusion | flops 2422210560 | bytes 16515072 | tf_op jit(solution)/shard_map/dot_general | solution.py:197
  399.3 7.5 %collective-permute-done.50 = bf16[256,768]{1,0:T(8,128)(2,1)} collective-permute-done((bf16[256,768]{1,0:T(8,128)(2,1)S(1)}, bf16[256,768]{1,0:T(8,128)(2,1)}, u32[]{:S(2)}, u32[]{:S(2)}) %collective-permute-start.50) | collective-permute-done | bytes 393248 | tf_op jit(solution)/shard_map/ppermute | solution.py:77
  415.4 3.7 collective-permute-done.52
  433.7 6.8 %convolution_add_fusion.3 = f32[1024,1536]{1,0:T(8,128)} fusion(f32[1024,1536]{1,0:T(8,128)} %convolution_add_fusion.4, bf16[1024,768]{1,0:T(8,128)(2,1)S(1)} %select_dynamic-update-slice_fusion.5, bf16[768,768]{1,0:T(8,128)(2,1)} %copy-done.51, bf16[768,768]{1,0:T(8,128)(2,1)S(1)} %copy-done.20), kind=kOutput, calls=%fused_computation.18 | convolution fusion | flops 2422210560 | bytes 16515072 | tf_op jit(solution)/shard_map/dot_general | solution.py:197
  440.8 9.3 %collective-permute-done.54 = bf16[256,768]{1,0:T(8,128)(2,1)S(1)} collective-permute-done((bf16[256,768]{1,0:T(8,128)(2,1)S(1)}, bf16[256,768]{1,0:T(8,128)(2,1)S(1)}, u32[]{:S(2)}, u32[]{:S(2)}) %collective-permute-start.54) | collective-permute-done | bytes 393248 | tf_op jit(solution)/shard_map/ppermute | solution.py:77
  452.3 7.1 %collective-permute-start.55 = (bf16[256,768]{1,0:T(8,128)(2,1)S(1)}, bf16[256,768]{1,0:T(8,128)(2,1)S(1)}, u32[]{:S(2)}, u32[]{:S(2)}) collective-permute-start(bf16[256,768]{1,0:T(8,128)(2,1)S(1)} %get-tuple-element.322), channel_id=1, source_target_pairs={{0,4},{12,8},{1,5},{13,9},{2,6},{14,10},{3,7},{15,11},{16,20},{28,... | collective-permute-start | bytes 1179656 | tf_op jit(solution)/shard_map/ppermute | solution.py:104
  462.1 5.5 collective-permute-done.55
  471.3 3.2 convolution_convert_fusion.2
  476.2 6.8 %convolution_add_fusion.2 = f32[1024,1536]{1,0:T(8,128)} fusion(f32[1024,1536]{1,0:T(8,128)} %convolution_add_fusion.3, bf16[1024,768]{1,0:T(8,128)(2,1)S(1)} %select_dynamic-update-slice_fusion.4, bf16[768,768]{1,0:T(8,128)(2,1)} %copy-done.50, bf16[768,768]{1,0:T(8,128)(2,1)S(1)} %copy-done.18), kind=kOutput, calls=%fused_computation.17 | convolution fusion | flops 2422210560 | bytes 16515072 | tf_op jit(solution)/shard_map/dot_general | solution.py:197
  492.3 3.3 convolution_convert_fusion.1
  497.7 6.8 %convolution_add_fusion.1 = f32[1024,1536]{1,0:T(8,128)} fusion(f32[1024,1536]{1,0:T(8,128)} %convolution_add_fusion.2, bf16[1024,768]{1,0:T(8,128)(2,1)S(1)} %select_dynamic-update-slice_fusion.3, bf16[768,768]{1,0:T(8,128)(2,1)} %collective-permute-done.28, bf16[768,768]{1,0:T(8,128)(2,1)S(1)} %copy-done.16), kind=kOutput, calls=%fused_computation.16 | convolution fusion | flops 2422210560 | bytes 16515072 | tf_op jit(solution)/shard_map/dot_general | solution.py:197
  507.2 11.3 %collective-permute-done.59 = bf16[768,768]{1,0:T(8,128)(2,1)} collective-permute-done((bf16[768,768]{1,0:T(8,128)(2,1)S(1)}, bf16[768,768]{1,0:T(8,128)(2,1)}, u32[]{:S(2)}, u32[]{:S(2)}) %collective-permute-start.59) | collective-permute-done | bytes 1179680 | tf_op jit(solution)/shard_map/ppermute | solution.py:104
  520.2 3.2 convolution_convert_fusion
  523.4 6.2 %convolution_add_fusion = f32[1024,1536]{1,0:T(8,128)S(1)} fusion(f32[1024,1536]{1,0:T(8,128)} %convolution_add_fusion.1, bf16[1024,768]{1,0:T(8,128)(2,1)S(1)} %select_dynamic-update-slice_fusion.2, bf16[768,768]{1,0:T(8,128)(2,1)} %collective-permute-done.35, bf16[768,768]{1,0:T(8,128)(2,1)S(1)} %copy-done.14), kind=kOutput, calls=%fused_computation.15 | convolution fusion | flops 2422210560 | bytes 16515072 | tf_op jit(solution)/shard_map/dot_general | solution.py:197
  534.8 3.6 pad_maximum_fusion
  550.0 14.5 %collective-permute-done.61 = bf16[256,1536]{1,0:T(8,128)(2,1)S(1)} collective-permute-done((bf16[256,1536]{1,0:T(8,128)(2,1)S(1)}, bf16[256,1536]{1,0:T(8,128)(2,1)S(1)}, u32[]{:S(2)}, u32[]{:S(2)}) %collective-permute-start.61) | collective-permute-done | bytes 786464 | tf_op jit(solution)/shard_map/ppermute | solution.py:25
  (402 shorter events, 229.9 us)
Async XLA Ops:
  0.6 20.9 %collective-permute-start.1 = (bf16[256,1536]{1,0:T(8,128)(2,1)}, bf16[256,1536]{1,0:T(8,128)(2,1)}, u32[]{:S(2)}, u32[]{:S(2)}) collective-permute-start(bf16[256,1536]{1,0:T(8,128)(2,1)} %param.36), channel_id=1, source_target_pairs={{0,2},{2,0},{1,3},{3,1},{4,6},{6,4},{5,7},{7,5},{8,10},{10,8},{9,1... | collective-permute-start | bytes 2359304 | tf_op jit(solution)/shard_map/ppermute | solution.py:25
  3.6 21.5 %collective-permute-start.2 = (bf16[256,1536]{1,0:T(8,128)(2,1)}, bf16[256,1536]{1,0:T(8,128)(2,1)}, u32[]{:S(2)}, u32[]{:S(2)}) collective-permute-start(bf16[256,1536]{1,0:T(8,128)(2,1)} %param.36), channel_id=1, source_target_pairs={{0,1},{1,0},{2,3},{3,2},{4,5},{5,4},{6,7},{7,6},{8,9},{9,8},{10,11... | collective-permute-start | bytes 2359304 | tf_op jit(solution)/shard_map/ppermute | solution.py:25
  7.0 56.8 %collective-permute-start = (bf16[128,6144]{1,0:T(8,128)(2,1)}, bf16[128,6144]{1,0:T(8,128)(2,1)}, u32[]{:S(2)}, u32[]{:S(2)}) collective-permute-start(bf16[128,6144]{1,0:T(8,128)(2,1)} %broadcast_select_fusion.4), channel_id=1, source_target_pairs={{0,1},{1,0},{2,3},{3,2},{4,5},{5,4},{6,7},{7,6},{8,9},{9,8},{10,11... | collective-permute-start | bytes 4718600 | tf_op jit(solution)/shard_map/ppermute | solution.py:25
  25.8 90.6 %collective-permute-start.15 = (bf16[768,768]{1,0:T(8,128)(2,1)}, bf16[768,768]{1,0:T(8,128)(2,1)}, u32[]{:S(2)}, u32[]{:S(2)}) collective-permute-start(bf16[768,768]{1,0:T(8,128)(2,1)} %get-tuple-element.343), channel_id=1, source_target_pairs={{0,1},{1,0},{2,3},{3,2},{4,5},{5,4},{6,7},{7,6},{8,9},{9,8},{10,11... | collective-permute-start | bytes 3538952 | tf_op jit(solution)/shard_map/ppermute | solution.py:25
  33.3 29.6 %collective-permute-start.5 = (bf16[768,768]{1,0:T(8,128)(2,1)S(1)}, bf16[768,768]{1,0:T(8,128)(2,1)S(1)}, u32[]{:S(2)}, u32[]{:S(2)}) collective-permute-start(bf16[768,768]{1,0:T(8,128)(2,1)S(1)} %constant_dynamic-slice_fusion.23), channel_id=1, source_target_pairs={{0,4},{12,8},{1,5},{13,9},{2,6},{14,10},{3,7},{15,11},{16,20},{28,... | collective-permute-start | bytes 3538952 | tf_op jit(solution)/shard_map/ppermute | solution.py:77
  65.5 33.8 %collective-permute-start.11 = (bf16[768,768]{1,0:T(8,128)(2,1)S(1)}, bf16[768,768]{1,0:T(8,128)(2,1)S(1)}, u32[]{:S(2)}, u32[]{:S(2)}) collective-permute-start(bf16[768,768]{1,0:T(8,128)(2,1)S(1)} %constant_dynamic-slice_fusion.22), channel_id=1, source_target_pairs={{0,4},{12,8},{1,5},{13,9},{2,6},{14,10},{3,7},{15,11},{16,20},{28,... | collective-permute-start | bytes 3538952 | tf_op jit(solution)/shard_map/ppermute | solution.py:77
  72.8 23.2 %collective-permute-start.8 = (bf16[256,768]{1,0:T(8,128)(2,1)S(1)}, bf16[256,768]{1,0:T(8,128)(2,1)S(1)}, u32[]{:S(2)}, u32[]{:S(2)}) collective-permute-start(bf16[256,768]{1,0:T(8,128)(2,1)S(1)} %add_convert_fusion.16), channel_id=1, source_target_pairs={{8,12},{4,0},{9,13},{5,1},{10,14},{6,2},{11,15},{7,3},{24,28},{20,... | collective-permute-start | bytes 1179656 | tf_op jit(solution)/shard_map/ppermute | solution.py:77
  100.6 23.2 %collective-permute-start.13 = (bf16[512,768]{1,0:T(8,128)(2,1)}, bf16[512,768]{1,0:T(8,128)(2,1)}, u32[]{:S(2)}, u32[]{:S(2)}) collective-permute-start(bf16[512,768]{1,0:T(8,128)(2,1)} %add_convert_fusion.7), channel_id=1, source_target_pairs={{4,8},{8,4},{5,9},{9,5},{6,10},{10,6},{7,11},{11,7},{20,24},{24,20... | collective-permute-start | bytes 2359304 | tf_op jit(solution)/shard_map/ppermute | solution.py:77
  105.6 87.4 %collective-permute-start.35 = (bf16[768,768]{1,0:T(8,128)(2,1)}, bf16[768,768]{1,0:T(8,128)(2,1)}, u32[]{:S(2)}, u32[]{:S(2)}) collective-permute-start(bf16[768,768]{1,0:T(8,128)(2,1)} %get-tuple-element.346), channel_id=1, source_target_pairs={{0,1},{1,0},{2,3},{3,2},{4,5},{5,4},{6,7},{7,6},{8,9},{9,8},{10,11... | collective-permute-start | bytes 3538952 | tf_op jit(solution)/shard_map/ppermute | solution.py:25
  105.6 44.5 %collective-permute-start.28 = (bf16[768,768]{1,0:T(8,128)(2,1)}, bf16[768,768]{1,0:T(8,128)(2,1)}, u32[]{:S(2)}, u32[]{:S(2)}) collective-permute-start(bf16[768,768]{1,0:T(8,128)(2,1)} %get-tuple-element.350), channel_id=1, source_target_pairs={{0,1},{1,0},{2,3},{3,2},{4,5},{5,4},{6,7},{7,6},{8,9},{9,8},{10,11... | collective-permute-start | bytes 3538952 | tf_op jit(solution)/shard_map/ppermute | solution.py:25
  118.4 27.2 %collective-permute-start.18 = (bf16[768,768]{1,0:T(8,128)(2,1)S(1)}, bf16[768,768]{1,0:T(8,128)(2,1)S(1)}, u32[]{:S(2)}, u32[]{:S(2)}) collective-permute-start(bf16[768,768]{1,0:T(8,128)(2,1)S(1)} %copy-done.49), channel_id=1, source_target_pairs={{0,4},{12,8},{1,5},{13,9},{2,6},{14,10},{3,7},{15,11},{16,20},{28,... | collective-permute-start | bytes 3538952 | tf_op jit(solution)/shard_map/ppermute | solution.py:77
  140.3 51.6 %collective-permute-start.17 = (bf16[768,768]{1,0:T(8,128)(2,1)S(1)}, bf16[768,768]{1,0:T(8,128)(2,1)S(1)}, u32[]{:S(2)}, u32[]{:S(2)}) collective-permute-start(bf16[768,768]{1,0:T(8,128)(2,1)S(1)} %copy-done.46), channel_id=1, source_target_pairs={{0,1},{1,0},{2,3},{3,2},{4,5},{5,4},{6,7},{7,6},{8,9},{9,8},{10,11... | collective-permute-start | bytes 3538952 | tf_op jit(solution)/shard_map/ppermute | solution.py:25
  153.5 37.4 %collective-permute-start.19 = (bf16[768,768]{1,0:T(8,128)(2,1)S(1)}, bf16[768,768]{1,0:T(8,128)(2,1)S(1)}, u32[]{:S(2)}, u32[]{:S(2)}) collective-permute-start(bf16[768,768]{1,0:T(8,128)(2,1)S(1)} %constant_dynamic-slice_fusion.18), channel_id=1, source_target_pairs={{0,4},{12,8},{1,5},{13,9},{2,6},{14,10},{3,7},{15,11},{16,20},{28,... | collective-permute-start | bytes 3538952 | tf_op jit(solution)/shard_map/ppermute | solution.py:77
  159.6 29.9 %collective-permute-start.21 = (bf16[512,768]{1,0:T(8,128)(2,1)S(1)}, bf16[512,768]{1,0:T(8,128)(2,1)S(1)}, u32[]{:S(2)}, u32[]{:S(2)}) collective-permute-start(bf16[512,768]{1,0:T(8,128)(2,1)S(1)} %constant_dynamic-slice_fusion.14), channel_id=1, source_target_pairs={{4,8},{8,4},{5,9},{9,5},{6,10},{10,6},{7,11},{11,7},{20,24},{24,20... | collective-permute-start | bytes 2359304 | tf_op jit(solution)/shard_map/ppermute | solution.py:104
  160.4 20.6 %collective-permute-start.23 = (bf16[256,768]{1,0:T(8,128)(2,1)S(1)}, bf16[256,768]{1,0:T(8,128)(2,1)S(1)}, u32[]{:S(2)}, u32[]{:S(2)}) collective-permute-start(bf16[256,768]{1,0:T(8,128)(2,1)S(1)} %add_convert_fusion.14), channel_id=1, source_target_pairs={{8,12},{4,0},{9,13},{5,1},{10,14},{6,2},{11,15},{7,3},{24,28},{20,... | collective-permute-start | bytes 1179656 | tf_op jit(solution)/shard_map/ppermute | solution.py:77
  182.2 22.5 %collective-permute-start.26 = (bf16[256,768]{1,0:T(8,128)(2,1)S(1)}, bf16[256,768]{1,0:T(8,128)(2,1)S(1)}, u32[]{:S(2)}, u32[]{:S(2)}) collective-permute-start(bf16[256,768]{1,0:T(8,128)(2,1)S(1)} %get-tuple-element.332), channel_id=1, source_target_pairs={{0,4},{12,8},{1,5},{13,9},{2,6},{14,10},{3,7},{15,11},{16,20},{28,... | collective-permute-start | bytes 1179656 | tf_op jit(solution)/shard_map/ppermute | solution.py:104
  196.4 30.8 %collective-permute-start.16 = (bf16[768,768]{1,0:T(8,128)(2,1)S(1)}, bf16[768,768]{1,0:T(8,128)(2,1)S(1)}, u32[]{:S(2)}, u32[]{:S(2)}) collective-permute-start(bf16[768,768]{1,0:T(8,128)(2,1)S(1)} %constant_dynamic-slice_fusion.17), channel_id=1, source_target_pairs={{8,12},{4,0},{9,13},{5,1},{10,14},{6,2},{11,15},{7,3},{24,28},{20,... | collective-permute-start | bytes 3538952 | tf_op jit(solution)/shard_map/ppermute | solution.py:104
  197.7 88.5 %collective-permute-start.27 = (bf16[768,768]{1,0:T(8,128)(2,1)}, bf16[768,768]{1,0:T(8,128)(2,1)}, u32[]{:S(2)}, u32[]{:S(2)}) collective-permute-start(bf16[768,768]{1,0:T(8,128)(2,1)} %constant_dynamic-slice_fusion.12), channel_id=1, source_target_pairs={{8,12},{4,0},{9,13},{5,1},{10,14},{6,2},{11,15},{7,3},{24,28},{20,... | collective-permute-start | bytes 3538952 | tf_op jit(solution)/shard_map/ppermute | solution.py:104
  199.0 63.3 %collective-permute-start.29 = (bf16[768,768]{1,0:T(8,128)(2,1)S(1)}, bf16[768,768]{1,0:T(8,128)(2,1)S(1)}, u32[]{:S(2)}, u32[]{:S(2)}) collective-permute-start(bf16[768,768]{1,0:T(8,128)(2,1)S(1)} %constant_dynamic-slice_fusion.13), channel_id=1, source_target_pairs={{0,4},{12,8},{1,5},{13,9},{2,6},{14,10},{3,7},{15,11},{16,20},{28,... | collective-permute-start | bytes 3538952 | tf_op jit(solution)/shard_map/ppermute | solution.py:77
  204.9 55.9 %collective-permute-start.30 = (bf16[512,768]{1,0:T(8,128)(2,1)S(1)}, bf16[512,768]{1,0:T(8,128)(2,1)S(1)}, u32[]{:S(2)}, u32[]{:S(2)}) collective-permute-start(bf16[512,768]{1,0:T(8,128)(2,1)S(1)} %constant_dynamic-slice_fusion.11), channel_id=1, source_target_pairs={{4,8},{8,4},{5,9},{9,5},{6,10},{10,6},{7,11},{11,7},{20,24},{24,20... | collective-permute-start | bytes 2359304 | tf_op jit(solution)/shard_map/ppermute | solution.py:104
  205.8 52.4 %collective-permute-start.31 = (bf16[256,768]{1,0:T(8,128)(2,1)S(1)}, bf16[256,768]{1,0:T(8,128)(2,1)S(1)}, u32[]{:S(2)}, u32[]{:S(2)}) collective-permute-start(bf16[256,768]{1,0:T(8,128)(2,1)S(1)} %add_convert_fusion.13), channel_id=1, source_target_pairs={{8,12},{4,0},{9,13},{5,1},{10,14},{6,2},{11,15},{7,3},{24,28},{20,... | collective-permute-start | bytes 1179656 | tf_op jit(solution)/shard_map/ppermute | solution.py:77
  236.3 37.0 %collective-permute-start.62 = (bf16[768,768]{1,0:T(8,128)(2,1)S(1)}, bf16[768,768]{1,0:T(8,128)(2,1)S(1)}, u32[]{:S(2)}, u32[]{:S(2)}) collective-permute-start(bf16[768,768]{1,0:T(8,128)(2,1)S(1)} %slice.749), channel_id=1, source_target_pairs={{0,1},{1,0},{2,3},{3,2},{4,5},{5,4},{6,7},{7,6},{8,9},{9,8},{10,11... | collective-permute-start | bytes 3538952 | tf_op jit(solution)/shard_map/ppermute | solution.py:25
  263.2 74.3 %collective-permute-start.34 = (bf16[768,768]{1,0:T(8,128)(2,1)}, bf16[768,768]{1,0:T(8,128)(2,1)}, u32[]{:S(2)}, u32[]{:S(2)}) collective-permute-start(bf16[768,768]{1,0:T(8,128)(2,1)} %constant_dynamic-slice_fusion.9), channel_id=1, source_target_pairs={{8,12},{4,0},{9,13},{5,1},{10,14},{6,2},{11,15},{7,3},{24,28},{20,... | collective-permute-start | bytes 3538952 | tf_op jit(solution)/shard_map/ppermute | solution.py:104
  266.8 46.2 %collective-permute-start.36 = (bf16[768,768]{1,0:T(8,128)(2,1)}, bf16[768,768]{1,0:T(8,128)(2,1)}, u32[]{:S(2)}, u32[]{:S(2)}) collective-permute-start(bf16[768,768]{1,0:T(8,128)(2,1)} %constant_dynamic-slice_fusion.10), channel_id=1, source_target_pairs={{0,4},{12,8},{1,5},{13,9},{2,6},{14,10},{3,7},{15,11},{16,20},{28,... | collective-permute-start | bytes 3538952 | tf_op jit(solution)/shard_map/ppermute | solution.py:77
  273.3 37.0 %collective-permute-start.37 = (bf16[512,768]{1,0:T(8,128)(2,1)}, bf16[512,768]{1,0:T(8,128)(2,1)}, u32[]{:S(2)}, u32[]{:S(2)}) collective-permute-start(bf16[512,768]{1,0:T(8,128)(2,1)} %constant_dynamic-slice_fusion.8), channel_id=1, source_target_pairs={{4,8},{8,4},{5,9},{9,5},{6,10},{10,6},{7,11},{11,7},{20,24},{24,20... | collective-permute-start | bytes 2359304 | tf_op jit(solution)/shard_map/ppermute | solution.py:104
  279.4 20.7 %collective-permute-start.38 = (bf16[256,768]{1,0:T(8,128)(2,1)S(1)}, bf16[256,768]{1,0:T(8,128)(2,1)}, u32[]{:S(2)}, u32[]{:S(2)}) collective-permute-start(bf16[256,768]{1,0:T(8,128)(2,1)S(1)} %add_convert_fusion.12), channel_id=1, source_target_pairs={{8,12},{4,0},{9,13},{5,1},{10,14},{6,2},{11,15},{7,3},{24,28},{20,... | collective-permute-start | bytes 1179656 | tf_op jit(solution)/shard_map/ppermute | solution.py:77
  292.7 33.2 %collective-permute-start.63 = (bf16[768,768]{1,0:T(8,128)(2,1)}, bf16[768,768]{1,0:T(8,128)(2,1)}, u32[]{:S(2)}, u32[]{:S(2)}) collective-permute-start(bf16[768,768]{1,0:T(8,128)(2,1)} %slice.751), channel_id=1, source_target_pairs={{0,1},{1,0},{2,3},{3,2},{4,5},{5,4},{6,7},{7,6},{8,9},{9,8},{10,11... | collective-permute-start | bytes 3538952 | tf_op jit(solution)/shard_map/ppermute | solution.py:25
  311.7 74.0 %collective-permute-start.41 = (bf16[768,768]{1,0:T(8,128)(2,1)}, bf16[768,768]{1,0:T(8,128)(2,1)}, u32[]{:S(2)}, u32[]{:S(2)}) collective-permute-start(bf16[768,768]{1,0:T(8,128)(2,1)} %constant_dynamic-slice_fusion.6), channel_id=1, source_target_pairs={{8,12},{4,0},{9,13},{5,1},{10,14},{6,2},{11,15},{7,3},{24,28},{20,... | collective-permute-start | bytes 3538952 | tf_op jit(solution)/shard_map/ppermute | solution.py:104
  319.3 45.2 %collective-permute-start.42 = (bf16[768,768]{1,0:T(8,128)(2,1)}, bf16[768,768]{1,0:T(8,128)(2,1)}, u32[]{:S(2)}, u32[]{:S(2)}) collective-permute-start(bf16[768,768]{1,0:T(8,128)(2,1)} %constant_dynamic-slice_fusion.7), channel_id=1, source_target_pairs={{0,4},{12,8},{1,5},{13,9},{2,6},{14,10},{3,7},{15,11},{16,20},{28,... | collective-permute-start | bytes 3538952 | tf_op jit(solution)/shard_map/ppermute | solution.py:77
  325.9 37.2 %collective-permute-start.43 = (bf16[512,768]{1,0:T(8,128)(2,1)}, bf16[512,768]{1,0:T(8,128)(2,1)}, u32[]{:S(2)}, u32[]{:S(2)}) collective-permute-start(bf16[512,768]{1,0:T(8,128)(2,1)} %constant_dynamic-slice_fusion.5), channel_id=1, source_target_pairs={{4,8},{8,4},{5,9},{9,5},{6,10},{10,6},{7,11},{11,7},{20,24},{24,20... | collective-permute-start | bytes 2359304 | tf_op jit(solution)/shard_map/ppermute | solution.py:104
  332.0 18.8 %collective-permute-start.44 = (bf16[256,768]{1,0:T(8,128)(2,1)S(1)}, bf16[256,768]{1,0:T(8,128)(2,1)}, u32[]{:S(2)}, u32[]{:S(2)}) collective-permute-start(bf16[256,768]{1,0:T(8,128)(2,1)S(1)} %add_convert_fusion.11), channel_id=1, source_target_pairs={{8,12},{4,0},{9,13},{5,1},{10,14},{6,2},{11,15},{7,3},{24,28},{20,... | collective-permute-start | bytes 1179656 | tf_op jit(solution)/shard_map/ppermute | solution.py:77
  343.4 35.2 %collective-permute-start.64 = (bf16[768,768]{1,0:T(8,128)(2,1)}, bf16[768,768]{1,0:T(8,128)(2,1)}, u32[]{:S(2)}, u32[]{:S(2)}) collective-permute-start(bf16[768,768]{1,0:T(8,128)(2,1)} %slice.755), channel_id=1, source_target_pairs={{0,1},{1,0},{2,3},{3,2},{4,5},{5,4},{6,7},{7,6},{8,9},{9,8},{10,11... | collective-permute-start | bytes 3538952 | tf_op jit(solution)/shard_map/ppermute | solution.py:25
  353.2 19.0 %collective-permute-start.46 = (bf16[256,768]{1,0:T(8,128)(2,1)S(1)}, bf16[256,768]{1,0:T(8,128)(2,1)S(1)}, u32[]{:S(2)}, u32[]{:S(2)}) collective-permute-start(bf16[256,768]{1,0:T(8,128)(2,1)S(1)} %get-tuple-element.326), channel_id=1, source_target_pairs={{0,4},{12,8},{1,5},{13,9},{2,6},{14,10},{3,7},{15,11},{16,20},{28,... | collective-permute-start | bytes 1179656 | tf_op jit(solution)/shard_map/ppermute | solution.py:104
  367.3 59.8 %collective-permute-start.47 = (bf16[768,768]{1,0:T(8,128)(2,1)}, bf16[768,768]{1,0:T(8,128)(2,1)}, u32[]{:S(2)}, u32[]{:S(2)}) collective-permute-start(bf16[768,768]{1,0:T(8,128)(2,1)} %constant_dynamic-slice_fusion.2), channel_id=1, source_target_pairs={{8,12},{4,0},{9,13},{5,1},{10,14},{6,2},{11,15},{7,3},{24,28},{20,... | collective-permute-start | bytes 3538952 | tf_op jit(solution)/shard_map/ppermute | solution.py:104
  372.1 41.2 %collective-permute-start.48 = (bf16[768,768]{1,0:T(8,128)(2,1)}, bf16[768,768]{1,0:T(8,128)(2,1)}, u32[]{:S(2)}, u32[]{:S(2)}) collective-permute-start(bf16[768,768]{1,0:T(8,128)(2,1)} %constant_dynamic-slice_fusion.4), channel_id=1, source_target_pairs={{0,4},{12,8},{1,5},{13,9},{2,6},{14,10},{3,7},{15,11},{16,20},{28,... | collective-permute-start | bytes 3538952 | tf_op jit(solution)/shard_map/ppermute | solution.py:77
  378.6 32.0 %collective-permute-start.49 = (bf16[512,768]{1,0:T(8,128)(2,1)}, bf16[512,768]{1,0:T(8,128)(2,1)}, u32[]{:S(2)}, u32[]{:S(2)}) collective-permute-start(bf16[512,768]{1,0:T(8,128)(2,1)} %constant_dynamic-slice_fusion.1), channel_id=1, source_target_pairs={{4,8},{8,4},{5,9},{9,5},{6,10},{10,6},{7,11},{11,7},{20,24},{24,20... | collective-permute-start | bytes 2359304 | tf_op jit(solution)/shard_map/ppermute | solution.py:104
  384.0 22.8 %collective-permute-start.50 = (bf16[256,768]{1,0:T(8,128)(2,1)S(1)}, bf16[256,768]{1,0:T(8,128)(2,1)}, u32[]{:S(2)}, u32[]{:S(2)}) collective-permute-start(bf16[256,768]{1,0:T(8,128)(2,1)S(1)} %add_convert_fusion.10), channel_id=1, source_target_pairs={{8,12},{4,0},{9,13},{5,1},{10,14},{6,2},{11,15},{7,3},{24,28},{20,... | collective-permute-start | bytes 1179656 | tf_op jit(solution)/shard_map/ppermute | solution.py:77
  391.9 29.9 %collective-permute-start.65 = (bf16[768,768]{1,0:T(8,128)(2,1)}, bf16[768,768]{1,0:T(8,128)(2,1)}, u32[]{:S(2)}, u32[]{:S(2)}) collective-permute-start(bf16[768,768]{1,0:T(8,128)(2,1)} %slice.759), channel_id=1, source_target_pairs={{0,1},{1,0},{2,3},{3,2},{4,5},{5,4},{6,7},{7,6},{8,9},{9,8},{10,11... | collective-permute-start | bytes 3538952 | tf_op jit(solution)/shard_map/ppermute | solution.py:25
  412.0 57.7 %collective-permute-start.53 = (bf16[768,768]{1,0:T(8,128)(2,1)}, bf16[768,768]{1,0:T(8,128)(2,1)}, u32[]{:S(2)}, u32[]{:S(2)}) collective-permute-start(bf16[768,768]{1,0:T(8,128)(2,1)} %constant_dynamic-slice_fusion), channel_id=1, source_target_pairs={{8,12},{4,0},{9,13},{5,1},{10,14},{6,2},{11,15},{7,3},{24,28},{20,... | collective-permute-start | bytes 3538952 | tf_op jit(solution)/shard_map/ppermute | solution.py:104
  420.1 39.3 %collective-permute-start.56 = (bf16[512,768]{1,0:T(8,128)(2,1)}, bf16[512,768]{1,0:T(8,128)(2,1)}, u32[]{:S(2)}, u32[]{:S(2)}) collective-permute-start(bf16[512,768]{1,0:T(8,128)(2,1)} %constant_dynamic-slice_fusion.16), channel_id=1, source_target_pairs={{4,8},{8,4},{5,9},{9,5},{6,10},{10,6},{7,11},{11,7},{20,24},{24,20... | collective-permute-start | bytes 2359304 | tf_op jit(solution)/shard_map/ppermute | solution.py:104
  425.6 24.5 %collective-permute-start.54 = (bf16[256,768]{1,0:T(8,128)(2,1)S(1)}, bf16[256,768]{1,0:T(8,128)(2,1)S(1)}, u32[]{:S(2)}, u32[]{:S(2)}) collective-permute-start(bf16[256,768]{1,0:T(8,128)(2,1)S(1)} %add_convert_fusion.9), channel_id=1, source_target_pairs={{8,12},{4,0},{9,13},{5,1},{10,14},{6,2},{11,15},{7,3},{24,28},{20,... | collective-permute-start | bytes 1179656 | tf_op jit(solution)/shard_map/ppermute | solution.py:77
  433.1 49.9 %collective-permute-start.66 = (bf16[768,768]{1,0:T(8,128)(2,1)}, bf16[768,768]{1,0:T(8,128)(2,1)}, u32[]{:S(2)}, u32[]{:S(2)}) collective-permute-start(bf16[768,768]{1,0:T(8,128)(2,1)} %slice.763), channel_id=1, source_target_pairs={{0,1},{1,0},{2,3},{3,2},{4,5},{5,4},{6,7},{7,6},{8,9},{9,8},{10,11... | collective-permute-start | bytes 3538952 | tf_op jit(solution)/shard_map/ppermute | solution.py:25
  460.8 29.7 %collective-permute-start.57 = (bf16[768,768]{1,0:T(8,128)(2,1)}, bf16[768,768]{1,0:T(8,128)(2,1)}, u32[]{:S(2)}, u32[]{:S(2)}) collective-permute-start(bf16[768,768]{1,0:T(8,128)(2,1)} %constant_dynamic-slice_fusion.3), channel_id=1, source_target_pairs={{8,12},{4,0},{9,13},{5,1},{10,14},{6,2},{11,15},{7,3},{24,28},{20,... | collective-permute-start | bytes 3538952 | tf_op jit(solution)/shard_map/ppermute | solution.py:104
  467.9 18.9 %collective-permute-start.58 = (bf16[512,768]{1,0:T(8,128)(2,1)S(1)}, bf16[512,768]{1,0:T(8,128)(2,1)}, u32[]{:S(2)}, u32[]{:S(2)}) collective-permute-start(bf16[512,768]{1,0:T(8,128)(2,1)S(1)} %constant_dynamic-slice_fusion.20), channel_id=1, source_target_pairs={{4,8},{8,4},{5,9},{9,5},{6,10},{10,6},{7,11},{11,7},{20,24},{24,20... | collective-permute-start | bytes 2359304 | tf_op jit(solution)/shard_map/ppermute | solution.py:104
  475.7 28.8 %collective-permute-start.67 = (bf16[768,768]{1,0:T(8,128)(2,1)}, bf16[768,768]{1,0:T(8,128)(2,1)S(1)}, u32[]{:S(2)}, u32[]{:S(2)}) collective-permute-start(bf16[768,768]{1,0:T(8,128)(2,1)} %slice.767), channel_id=1, source_target_pairs={{0,1},{1,0},{2,3},{3,2},{4,5},{5,4},{6,7},{7,6},{8,9},{9,8},{10,11... | collective-permute-start | bytes 3538952 | tf_op jit(solution)/shard_map/ppermute | solution.py:25
  487.2 31.3 %collective-permute-start.59 = (bf16[768,768]{1,0:T(8,128)(2,1)S(1)}, bf16[768,768]{1,0:T(8,128)(2,1)}, u32[]{:S(2)}, u32[]{:S(2)}) collective-permute-start(bf16[768,768]{1,0:T(8,128)(2,1)S(1)} %constant_dynamic-slice_fusion.15), channel_id=1, source_target_pairs={{8,12},{4,0},{9,13},{5,1},{10,14},{6,2},{11,15},{7,3},{24,28},{20,... | collective-permute-start | bytes 3538952 | tf_op jit(solution)/shard_map/ppermute | solution.py:104
  496.7 42.1 %collective-permute-start.68 = (bf16[768,768]{1,0:T(8,128)(2,1)}, bf16[768,768]{1,0:T(8,128)(2,1)}, u32[]{:S(2)}, u32[]{:S(2)}) collective-permute-start(bf16[768,768]{1,0:T(8,128)(2,1)} %slice.771), channel_id=1, source_target_pairs={{0,1},{1,0},{2,3},{3,2},{4,5},{5,4},{6,7},{7,6},{8,9},{9,8},{10,11... | collective-permute-start | bytes 3538952 | tf_op jit(solution)/shard_map/ppermute | solution.py:25
  544.9 19.5 %collective-permute-start.61 = (bf16[256,1536]{1,0:T(8,128)(2,1)S(1)}, bf16[256,1536]{1,0:T(8,128)(2,1)S(1)}, u32[]{:S(2)}, u32[]{:S(2)}) collective-permute-start(bf16[256,1536]{1,0:T(8,128)(2,1)S(1)} %select_convert_fusion.1), channel_id=1, source_target_pairs={{0,2},{2,0},{1,3},{3,1},{4,6},{6,4},{5,7},{7,5},{8,10},{10,8},{9,1... | collective-permute-start | bytes 2359304 | tf_op jit(solution)/shard_map/ppermute | solution.py:25
  (83 other events, 772.8 us)

commit v2 on v1

--- a/solution.py
+++ b/solution.py
@@ -43,9 +43,9 @@
 
 
 def pieces(half, nx):
-    count = 8 if nx <= 4 else 2
-    width = half // count
-    return [(c * width, width) for c in range(count)]
+    shares = (1, 1, 1, 1, 1, 1, 1, 1) if nx <= 4 else (1, 1)
+    widths = [half * share // sum(shares) for share in shares]
+    return [(sum(widths[:c]), widths[c]) for c in range(len(widths))]
 
 
 def after(value, *others):
@@ -139,7 +139,7 @@
     bias_own = bias_own.astype(F32)
 
     weight_grad = jnp.zeros((mine, hidden), BF16)
-    input_sum = jnp.zeros((tokens.shape[0], features), F32)
+    input_sum = jnp.zeros((tokens.shape[0], features), BF16)
     chunks = pieces(half, nx)
     count, steps = len(chunks), nx - 1
     lines = [Line(nx, rank, block) for _ in chunks]
@@ -194,9 +194,8 @@
         bias_sums.append(jnp.sum(grad, axis=0, dtype=F32))
         w_grad = lax.dot_general(tokens, grad, (((0,), (0,)), ((), ())), preferred_element_type=F32).astype(BF16)
         w_own, w_other = w_grad[:mine], swap(w_grad[mine:], "gz")
-        input_sum = input_sum + lax.dot_general(
-            grad, weights[c], (((1,), (1,)), ((), ())), preferred_element_type=F32
-        )
+        term = lax.dot_general(grad, weights[c], (((1,), (1,)), ((), ())), preferred_element_type=F32)
+        input_sum = (input_sum.astype(F32) + term).astype(BF16)
         note(w_grad, input_sum)
         weight_grad = weight_grad.at[:, start : start + width].set(by_core(core, w_own, w_other))
         weight_grad = weight_grad.at[:, half + start : half + start + width].set(by_core(core, w_other, w_own))
@@ -210,8 +209,8 @@
         for i in range(count + 4):
             do(reduce_start, i)
             do(gather_next, i - 2, 1)
+            do(multiply, i + 1)
             do(reduce_next, i - 1, 2)
-            do(multiply, i + 1)
             do(use, i - 4)
             do(slope, i - 1)
             do(gather_next, i - 2, 2)
@@ -231,6 +230,7 @@
     bias_other = swap(bias_own, "gz")
     bias_grad = jnp.concatenate([by_core(core, bias_own, bias_other), by_core(core, bias_other, bias_own)])
 
+    input_sum = input_sum.astype(F32)
     input_sum = jnp.concatenate(
         [
             by_core(core, input_sum[:, :mine], input_sum[:, mine:]),

time: 575 us -> 553 us (0.962)
  matrix products: 107 us -> 92 us
  starting transfers between devices: 139 us -> 126 us
  waiting for transfers between devices: 150 us -> 163 us
    ppermute x24, starting transfers between devices: 62.8 us -> 42.3 us  [gather_permute(): lax.ppermute(send, 'gx', [(u, u + 1), (n - 1 - u, n - 2 - u)])]
    dot_general x8, matrix products: 55 us -> 43.6 us  [use(): lax.dot_general(grad, weights[c], (((1,), (1,)), ((), ())), preferred_ele...]
    ppermute x24, starting transfers between devices: 67.7 us -> 77.5 us  [reduce_permute(): lax.ppermute(send, 'gx', [(s, s + 1), (n - 1 - s, n - 2 - s)])]
    ppermute x24, waiting for transfers between devices: 84.9 us -> 94.1 us  [reduce_permute(): lax.ppermute(send, 'gx', [(s, s + 1), (n - 1 - s, n - 2 - s)])]
    unnamed x127 -> x129, local copies, waits for them, and re-layouts: 12 us -> 12.7 us
  transfers between devices with their start and end apart: 71 -> 71, of which waited for: 19 -> 23; matrix products, arithmetic and copies ran while one was open for 46% -> 44% of each run, Pallas kernels for 0% -> 0%
where the time goes in v2:
time: 553 us; the launch traced here: 542 us
  waiting for transfers between devices  163 us (29%)
  starting transfers between devices  126 us (23%)
  other arithmetic  118 us (21%)
  matrix products  92 us (17%)
  local copies, waits for them, and re-layouts  40.5 us (7%)
    ppermute x24, waiting for transfers between devices, reduce_permute(): lax.ppermute(send, 'gx', [(s, s + 1), (n - 1 - s, n - 2 - s)])  94.1 us
    ppermute x24, starting transfers between devices, reduce_permute(): lax.ppermute(send, 'gx', [(s, s + 1), (n - 1 - s, n - 2 - s)])  77.5 us
    ppermute x24, waiting for transfers between devices, gather_permute(): lax.ppermute(send, 'gx', [(u, u + 1), (n - 1 - u, n - 2 - u)])  52.5 us
    dot_general x8, matrix products, use(): lax.dot_general(grad, weights[c], (((1,), (1,)), ((), ())), preferred_ele...  43.6 us
    ppermute x24, starting transfers between devices, gather_permute(): lax.ppermute(send, 'gx', [(u, u + 1), (n - 1 - u, n - 2 - u)])  42.3 us
    dot_general x8, matrix products, use(): lax.dot_general(tokens, grad, (((0,), (0,)), ((), ())), preferred_element...  26.3 us
    select_n x9, other arithmetic, by_core(): return jnp.where(core == 0, first, second)  23.2 us
    dot_general x8, matrix products, multiply(): jnp.dot(tokens, ordered(w), preferred_element_type=F32).astype(BF16)  22.1 us
  transfers between devices with their start and end apart: 71, of which 23 were waited for; matrix products, arithmetic and copies ran while one was open for 44% of the time, Pallas kernels for 0%

profile of v2, /device:TPU:0, one launch (start us, length us, event | category | flops | bytes accessed | tf_op | source)
XLA Modules:
  0.0 542.4 jit_solution(14137773220137676280)
XLA Ops:
  0.6 3.0 collective-permute-start.1
  3.6 6.9 %broadcast_select_fusion.10 = (bf16[768,768]{1,0:T(8,128)(2,1)}, bf16[768,768]{1,0:T(8,128)(2,1)}, bf16[768,768]{1,0:T(8,128)(2,1)}, bf16[768,768]{1,0:T(8,128)(...) fusion(pred[]{:T(512)S(6)} %eq.13, bf16[768,12288]{1,0:T(8,128)(2,1)} %param.37), kind=kLoop, calls=%fused_computation.138 | loop fusion | flops 4128768 | bytes 17694720 | tf_op jit(solution)/shard_map/jit(_where)/select_n | solution.py:21
  11.1 8.9 %broadcast_select_fusion.11 = (bf16[768,768]{1,0:T(8,128)(2,1)}, bf16[768,768]{1,0:T(8,128)(2,1)}, bf16[768,768]{1,0:T(8,128)(2,1)}, bf16[768,768]{1,0:T(8,128)(...) fusion(pred[]{:T(512)S(6)} %eq.13, ...), kind=kLoop, calls=%fused_computation.139 | loop fusion | flops 5308416 | bytes 22413312 | tf_op jit(solution)/shard_map/jit(_where)/select_n | solution.py:21
  30.0 3.9 convolution_convert_fusion.16
  36.2 4.5 collective-permute-start.5
  56.6 9.1 %collective-permute-done.5 = bf16[768,768]{1,0:T(8,128)(2,1)} collective-permute-done((bf16[768,768]{1,0:T(8,128)(2,1)}, bf16[768,768]{1,0:T(8,128)(2,1)}, u32[]{:S(2)}, u32[]{:S(2)}) %collective-permute-start.5) | collective-permute-done | bytes 1179680 | tf_op jit(solution)/shard_map/ppermute | solution.py:77
  72.0 21.4 %collective-permute-start.11 = (bf16[768,768]{1,0:T(8,128)(2,1)S(1)}, bf16[768,768]{1,0:T(8,128)(2,1)S(1)}, u32[]{:S(2)}, u32[]{:S(2)}) collective-permute-start(bf16[768,768]{1,0:T(8,128)(2,1)S(1)} %constant_dynamic-slice_fusion.22), channel_id=1, source_target_pairs={{0,4},{12,8},{1,5},{13,9},{2,6},{14,10},{3,7},{15,11},{16,20},{28,... | collective-permute-start | bytes 3538952 | tf_op jit(solution)/shard_map/ppermute | solution.py:77
  97.1 8.9 %collective-permute-done.9 = bf16[256,768]{1,0:T(8,128)(2,1)S(1)} collective-permute-done((bf16[256,768]{1,0:T(8,128)(2,1)S(1)}, bf16[256,768]{1,0:T(8,128)(2,1)S(1)}, u32[]{:S(2)}, u32[]{:S(2)}) %collective-permute-start.9) | collective-permute-done | bytes 393248 | tf_op jit(solution)/shard_map/ppermute | solution.py:77
  111.3 8.4 %collective-permute-done.11 = bf16[768,768]{1,0:T(8,128)(2,1)S(1)} collective-permute-done((bf16[768,768]{1,0:T(8,128)(2,1)S(1)}, bf16[768,768]{1,0:T(8,128)(2,1)S(1)}, u32[]{:S(2)}, u32[]{:S(2)}) %collective-permute-start.11) | collective-permute-done | bytes 1179680 | tf_op jit(solution)/shard_map/ppermute | solution.py:77
  120.6 6.2 %collective-permute-done.10 = bf16[256,768]{1,0:T(8,128)(2,1)S(1)} collective-permute-done((bf16[256,768]{1,0:T(8,128)(2,1)S(1)}, bf16[256,768]{1,0:T(8,128)(2,1)S(1)}, u32[]{:S(2)}, u32[]{:S(2)}) %collective-permute-start.10) | collective-permute-done | bytes 393248 | tf_op jit(solution)/shard_map/ppermute | solution.py:104
  126.9 4.4 collective-permute-start.17
  138.8 13.1 %collective-permute-done.15 = bf16[256,768]{1,0:T(8,128)(2,1)S(1)} collective-permute-done((bf16[256,768]{1,0:T(8,128)(2,1)S(1)}, bf16[256,768]{1,0:T(8,128)(2,1)S(1)}, u32[]{:S(2)}, u32[]{:S(2)}) %collective-permute-start.15) | collective-permute-done | bytes 393248 | tf_op jit(solution)/shard_map/ppermute | solution.py:77
  158.6 7.2 %collective-permute-start.18 = (bf16[768,768]{1,0:T(8,128)(2,1)S(1)}, bf16[768,768]{1,0:T(8,128)(2,1)S(1)}, u32[]{:S(2)}, u32[]{:S(2)}) collective-permute-start(bf16[768,768]{1,0:T(8,128)(2,1)S(1)} %constant_dynamic-slice_fusion.18), channel_id=1, source_target_pairs={{0,4},{12,8},{1,5},{13,9},{2,6},{14,10},{3,7},{15,11},{16,20},{28,... | collective-permute-start | bytes 3538952 | tf_op jit(solution)/shard_map/ppermute | solution.py:77
  175.8 18.3 %collective-permute-done.23 = bf16[256,768]{1,0:T(8,128)(2,1)S(1)} collective-permute-done((bf16[256,768]{1,0:T(8,128)(2,1)S(1)}, bf16[256,768]{1,0:T(8,128)(2,1)S(1)}, u32[]{:S(2)}, u32[]{:S(2)}) %collective-permute-start.23) | collective-permute-done | bytes 393248 | tf_op jit(solution)/shard_map/ppermute | solution.py:77
  200.5 5.7 %collective-permute-start.28 = (bf16[768,768]{1,0:T(8,128)(2,1)S(1)}, bf16[768,768]{1,0:T(8,128)(2,1)S(1)}, u32[]{:S(2)}, u32[]{:S(2)}) collective-permute-start(bf16[768,768]{1,0:T(8,128)(2,1)S(1)} %constant_dynamic-slice_fusion.13), channel_id=1, source_target_pairs={{0,4},{12,8},{1,5},{13,9},{2,6},{14,10},{3,7},{15,11},{16,20},{28,... | collective-permute-start | bytes 3538952 | tf_op jit(solution)/shard_map/ppermute | solution.py:77
  212.3 7.1 %collective-permute-done.16 = bf16[768,768]{1,0:T(8,128)(2,1)S(1)} collective-permute-done((bf16[768,768]{1,0:T(8,128)(2,1)S(1)}, bf16[768,768]{1,0:T(8,128)(2,1)S(1)}, u32[]{:S(2)}, u32[]{:S(2)}) %collective-permute-start.16) | collective-permute-done | bytes 1179680 | tf_op jit(solution)/shard_map/ppermute | solution.py:104
  219.8 3.3 convolution_convert_fusion.8
  224.6 5.3 convolution_convert_fusion
  229.9 12.9 %collective-permute-done.30 = bf16[256,768]{1,0:T(8,128)(2,1)S(1)} collective-permute-done((bf16[256,768]{1,0:T(8,128)(2,1)S(1)}, bf16[256,768]{1,0:T(8,128)(2,1)S(1)}, u32[]{:S(2)}, u32[]{:S(2)}) %collective-permute-start.30) | collective-permute-done | bytes 393248 | tf_op jit(solution)/shard_map/ppermute | solution.py:77
  249.1 5.9 %collective-permute-done.33 = bf16[256,768]{1,0:T(8,128)(2,1)S(1)} collective-permute-done((bf16[256,768]{1,0:T(8,128)(2,1)S(1)}, bf16[256,768]{1,0:T(8,128)(2,1)S(1)}, u32[]{:S(2)}, u32[]{:S(2)}) %collective-permute-start.33) | collective-permute-done | bytes 393248 | tf_op jit(solution)/shard_map/ppermute | solution.py:104
  255.0 5.4 collective-permute-start.35
  275.7 3.3 convolution_convert_fusion.7
  280.0 6.1 %add_convert_fusion.6 = bf16[1024,1536]{1,0:T(8,128)(2,1)} fusion(bf16[1024,1536]{1,0:T(8,128)(2,1)} %convolution_convert_fusion, bf16[1024,768]{1,0:T(8,128)(2,1)S(1)} %select_dynamic-update-slice_fusion.8, bf16[768,768]{1,0:T(8,128)(2,1)} %collective-permute-done.6, bf16[768,768]{1,0:T(8,128)(2,1)} %get-tuple-element.338), kind=kOutput, calls=%fused_computation.7 | convolution fusion | flops 2425356288 | bytes 10223616 | tf_op jit(solution)/shard_map/dot_general | solution.py:197
  289.8 4.0 collective-permute-start.40
  298.9 3.9 collective-permute-done.40
  302.8 5.4 %collective-permute-start.42 = (bf16[768,768]{1,0:T(8,128)(2,1)}, bf16[768,768]{1,0:T(8,128)(2,1)}, u32[]{:S(2)}, u32[]{:S(2)}) collective-permute-start(bf16[768,768]{1,0:T(8,128)(2,1)} %constant_dynamic-slice_fusion.7), channel_id=1, source_target_pairs={{0,4},{12,8},{1,5},{13,9},{2,6},{14,10},{3,7},{15,11},{16,20},{28,... | collective-permute-start | bytes 3538952 | tf_op jit(solution)/shard_map/ppermute | solution.py:77
  323.9 3.3 convolution_convert_fusion.6
  328.3 6.1 %add_convert_fusion.5 = bf16[1024,1536]{1,0:T(8,128)(2,1)} fusion(bf16[1024,1536]{1,0:T(8,128)(2,1)} %add_convert_fusion.6, bf16[1024,768]{1,0:T(8,128)(2,1)S(1)} %select_dynamic-update-slice_fusion.7, bf16[768,768]{1,0:T(8,128)(2,1)} %collective-permute-done.8, bf16[768,768]{1,0:T(8,128)(2,1)} %get-tuple-element.340), kind=kOutput, calls=%fused_computation.6 | convolution fusion | flops 2425356288 | bytes 10223616 | tf_op jit(solution)/shard_map/dot_general | solution.py:197
  346.8 4.2 collective-permute-done.46
  351.0 5.4 collective-permute-start.48
  366.9 3.3 convolution_convert_fusion.5
  371.2 6.1 %add_convert_fusion.4 = bf16[1024,1536]{1,0:T(8,128)(2,1)} fusion(bf16[1024,1536]{1,0:T(8,128)(2,1)} %add_convert_fusion.5, bf16[1024,768]{1,0:T(8,128)(2,1)S(1)} %select_dynamic-update-slice_fusion.6, bf16[768,768]{1,0:T(8,128)(2,1)} %collective-permute-done.14, bf16[768,768]{1,0:T(8,128)(2,1)} %get-tuple-element.342), kind=kOutput, calls=%fused_computation.5 | convolution fusion | flops 2425356288 | bytes 10223616 | tf_op jit(solution)/shard_map/dot_general | solution.py:197
  377.7 7.4 %collective-permute-done.50 = bf16[256,768]{1,0:T(8,128)(2,1)} collective-permute-done((bf16[256,768]{1,0:T(8,128)(2,1)}, bf16[256,768]{1,0:T(8,128)(2,1)}, u32[]{:S(2)}, u32[]{:S(2)}) %collective-permute-start.50) | collective-permute-done | bytes 393248 | tf_op jit(solution)/shard_map/ppermute | solution.py:77
  393.9 3.4 collective-permute-done.52
  406.9 3.3 convolution_convert_fusion.4
  411.9 5.8 %add_convert_fusion.3 = bf16[1024,1536]{1,0:T(8,128)(2,1)} fusion(bf16[1024,1536]{1,0:T(8,128)(2,1)} %add_convert_fusion.4, bf16[1024,768]{1,0:T(8,128)(2,1)S(1)} %select_dynamic-update-slice_fusion.5, bf16[768,768]{1,0:T(8,128)(2,1)} %copy-done.57, bf16[768,768]{1,0:T(8,128)(2,1)S(1)} %copy-done.16), kind=kOutput, calls=%fused_computation.4 | convolution fusion | flops 2425356288 | bytes 10223616 | tf_op jit(solution)/shard_map/dot_general | solution.py:197
  418.0 10.7 %collective-permute-done.54 = bf16[256,768]{1,0:T(8,128)(2,1)} collective-permute-done((bf16[256,768]{1,0:T(8,128)(2,1)S(1)}, bf16[256,768]{1,0:T(8,128)(2,1)}, u32[]{:S(2)}, u32[]{:S(2)}) %collective-permute-start.54) | collective-permute-done | bytes 393248 | tf_op jit(solution)/shard_map/ppermute | solution.py:77
  431.0 7.1 %collective-permute-start.55 = (bf16[256,768]{1,0:T(8,128)(2,1)S(1)}, bf16[256,768]{1,0:T(8,128)(2,1)S(1)}, u32[]{:S(2)}, u32[]{:S(2)}) collective-permute-start(bf16[256,768]{1,0:T(8,128)(2,1)S(1)} %get-tuple-element.322), channel_id=1, source_target_pairs={{0,4},{12,8},{1,5},{13,9},{2,6},{14,10},{3,7},{15,11},{16,20},{28,... | collective-permute-start | bytes 1179656 | tf_op jit(solution)/shard_map/ppermute | solution.py:104
  440.9 5.7 %collective-permute-done.55 = bf16[256,768]{1,0:T(8,128)(2,1)S(1)} collective-permute-done((bf16[256,768]{1,0:T(8,128)(2,1)S(1)}, bf16[256,768]{1,0:T(8,128)(2,1)S(1)}, u32[]{:S(2)}, u32[]{:S(2)}) %collective-permute-start.55) | collective-permute-done | bytes 393248 | tf_op jit(solution)/shard_map/ppermute | solution.py:104
  450.4 3.3 convolution_convert_fusion.3
  455.4 5.8 %add_convert_fusion.2 = bf16[1024,1536]{1,0:T(8,128)(2,1)} fusion(bf16[1024,1536]{1,0:T(8,128)(2,1)} %add_convert_fusion.3, bf16[1024,768]{1,0:T(8,128)(2,1)S(1)} %select_dynamic-update-slice_fusion.4, bf16[768,768]{1,0:T(8,128)(2,1)} %copy-done.54, bf16[768,768]{1,0:T(8,128)(2,1)S(1)} %copy-done.14), kind=kOutput, calls=%fused_computation.3 | convolution fusion | flops 2425356288 | bytes 10223616 | tf_op jit(solution)/shard_map/dot_general | solution.py:197
  471.0 3.3 convolution_convert_fusion.2
  476.1 5.8 %add_convert_fusion.1 = bf16[1024,1536]{1,0:T(8,128)(2,1)} fusion(bf16[1024,1536]{1,0:T(8,128)(2,1)} %add_convert_fusion.2, bf16[1024,768]{1,0:T(8,128)(2,1)S(1)} %select_dynamic-update-slice_fusion.3, bf16[768,768]{1,0:T(8,128)(2,1)} %copy-done.53, bf16[768,768]{1,0:T(8,128)(2,1)S(1)} %copy-done.12), kind=kOutput, calls=%fused_computation.2 | convolution fusion | flops 2425356288 | bytes 10223616 | tf_op jit(solution)/shard_map/dot_general | solution.py:197
  484.5 13.0 %collective-permute-done.59 = bf16[768,768]{1,0:T(8,128)(2,1)} collective-permute-done((bf16[768,768]{1,0:T(8,128)(2,1)S(1)}, bf16[768,768]{1,0:T(8,128)(2,1)}, u32[]{:S(2)}, u32[]{:S(2)}) %collective-permute-start.59) | collective-permute-done | bytes 1179680 | tf_op jit(solution)/shard_map/ppermute | solution.py:104
  499.5 3.5 convolution_convert_fusion.1
  508.6 3.2 slice_select_fusion.2
  511.8 3.6 pad_maximum_fusion
  526.3 14.4 %collective-permute-done.61 = bf16[256,1536]{1,0:T(8,128)(2,1)S(1)} collective-permute-done((bf16[256,1536]{1,0:T(8,128)(2,1)S(1)}, bf16[256,1536]{1,0:T(8,128)(2,1)S(1)}, u32[]{:S(2)}, u32[]{:S(2)}) %collective-permute-start.61) | collective-permute-done | bytes 786464 | tf_op jit(solution)/shard_map/ppermute | solution.py:25
  (404 shorter events, 219.5 us)
Async XLA Ops:
  0.6 20.9 %collective-permute-start.1 = (bf16[256,1536]{1,0:T(8,128)(2,1)}, bf16[256,1536]{1,0:T(8,128)(2,1)}, u32[]{:S(2)}, u32[]{:S(2)}) collective-permute-start(bf16[256,1536]{1,0:T(8,128)(2,1)} %param.36), channel_id=1, source_target_pairs={{0,2},{2,0},{1,3},{3,1},{4,6},{6,4},{5,7},{7,5},{8,10},{10,8},{9,1... | collective-permute-start | bytes 2359304 | tf_op jit(solution)/shard_map/ppermute | solution.py:25
  3.6 20.7 %collective-permute-start.2 = (bf16[256,1536]{1,0:T(8,128)(2,1)}, bf16[256,1536]{1,0:T(8,128)(2,1)}, u32[]{:S(2)}, u32[]{:S(2)}) collective-permute-start(bf16[256,1536]{1,0:T(8,128)(2,1)} %param.36), channel_id=1, source_target_pairs={{0,1},{1,0},{2,3},{3,2},{4,5},{5,4},{6,7},{7,6},{8,9},{9,8},{10,11... | collective-permute-start | bytes 2359304 | tf_op jit(solution)/shard_map/ppermute | solution.py:25
  19.9 31.3 %collective-permute-start.6 = (bf16[768,768]{1,0:T(8,128)(2,1)}, bf16[768,768]{1,0:T(8,128)(2,1)}, u32[]{:S(2)}, u32[]{:S(2)}) collective-permute-start(bf16[768,768]{1,0:T(8,128)(2,1)} %get-tuple-element.339), channel_id=1, source_target_pairs={{0,1},{1,0},{2,3},{3,2},{4,5},{5,4},{6,7},{7,6},{8,9},{9,8},{10,11... | collective-permute-start | bytes 3538952 | tf_op jit(solution)/shard_map/ppermute | solution.py:25
  20.0 47.1 %collective-permute-start.8 = (bf16[768,768]{1,0:T(8,128)(2,1)}, bf16[768,768]{1,0:T(8,128)(2,1)}, u32[]{:S(2)}, u32[]{:S(2)}) collective-permute-start(bf16[768,768]{1,0:T(8,128)(2,1)} %get-tuple-element.341), channel_id=1, source_target_pairs={{0,1},{1,0},{2,3},{3,2},{4,5},{5,4},{6,7},{7,6},{8,9},{9,8},{10,11... | collective-permute-start | bytes 3538952 | tf_op jit(solution)/shard_map/ppermute | solution.py:25
  24.3 69.2 %collective-permute-start = (bf16[128,6144]{1,0:T(8,128)(2,1)}, bf16[128,6144]{1,0:T(8,128)(2,1)}, u32[]{:S(2)}, u32[]{:S(2)}) collective-permute-start(bf16[128,6144]{1,0:T(8,128)(2,1)} %broadcast_select_fusion.4), channel_id=1, source_target_pairs={{0,1},{1,0},{2,3},{3,2},{4,5},{5,4},{6,7},{7,6},{8,9},{9,8},{10,11... | collective-permute-start | bytes 4718600 | tf_op jit(solution)/shard_map/ppermute | solution.py:25
  26.0 82.4 %collective-permute-start.14 = (bf16[768,768]{1,0:T(8,128)(2,1)}, bf16[768,768]{1,0:T(8,128)(2,1)}, u32[]{:S(2)}, u32[]{:S(2)}) collective-permute-start(bf16[768,768]{1,0:T(8,128)(2,1)} %get-tuple-element.343), channel_id=1, source_target_pairs={{0,1},{1,0},{2,3},{3,2},{4,5},{5,4},{6,7},{7,6},{8,9},{9,8},{10,11... | collective-permute-start | bytes 3538952 | tf_op jit(solution)/shard_map/ppermute | solution.py:25
  36.2 29.5 %collective-permute-start.5 = (bf16[768,768]{1,0:T(8,128)(2,1)}, bf16[768,768]{1,0:T(8,128)(2,1)}, u32[]{:S(2)}, u32[]{:S(2)}) collective-permute-start(bf16[768,768]{1,0:T(8,128)(2,1)} %constant_dynamic-slice_fusion.23), channel_id=1, source_target_pairs={{0,4},{12,8},{1,5},{13,9},{2,6},{14,10},{3,7},{15,11},{16,20},{28,... | collective-permute-start | bytes 3538952 | tf_op jit(solution)/shard_map/ppermute | solution.py:77
  51.2 84.0 %collective-permute-start.22 = (bf16[768,768]{1,0:T(8,128)(2,1)}, bf16[768,768]{1,0:T(8,128)(2,1)S(1)}, u32[]{:S(2)}, u32[]{:S(2)}) collective-permute-start(bf16[768,768]{1,0:T(8,128)(2,1)} %get-tuple-element.345), channel_id=1, source_target_pairs={{0,1},{1,0},{2,3},{3,2},{4,5},{5,4},{6,7},{7,6},{8,9},{9,8},{10,11... | collective-permute-start | bytes 3538952 | tf_op jit(solution)/shard_map/ppermute | solution.py:25
  65.7 71.0 %collective-permute-start.25 = (bf16[768,768]{1,0:T(8,128)(2,1)S(1)}, bf16[768,768]{1,0:T(8,128)(2,1)S(1)}, u32[]{:S(2)}, u32[]{:S(2)}) collective-permute-start(bf16[768,768]{1,0:T(8,128)(2,1)S(1)} %copy-done.52), channel_id=1, source_target_pairs={{0,1},{1,0},{2,3},{3,2},{4,5},{5,4},{6,7},{7,6},{8,9},{9,8},{10,11... | collective-permute-start | bytes 3538952 | tf_op jit(solution)/shard_map/ppermute | solution.py:25
  72.0 47.7 %collective-permute-start.11 = (bf16[768,768]{1,0:T(8,128)(2,1)S(1)}, bf16[768,768]{1,0:T(8,128)(2,1)S(1)}, u32[]{:S(2)}, u32[]{:S(2)}) collective-permute-start(bf16[768,768]{1,0:T(8,128)(2,1)S(1)} %constant_dynamic-slice_fusion.22), channel_id=1, source_target_pairs={{0,4},{12,8},{1,5},{13,9},{2,6},{14,10},{3,7},{15,11},{16,20},{28,... | collective-permute-start | bytes 3538952 | tf_op jit(solution)/shard_map/ppermute | solution.py:77
  106.0 65.3 %collective-permute-start.32 = (bf16[768,768]{1,0:T(8,128)(2,1)S(1)}, bf16[768,768]{1,0:T(8,128)(2,1)S(1)}, u32[]{:S(2)}, u32[]{:S(2)}) collective-permute-start(bf16[768,768]{1,0:T(8,128)(2,1)S(1)} %copy-done.51), channel_id=1, source_target_pairs={{0,1},{1,0},{2,3},{3,2},{4,5},{5,4},{6,7},{7,6},{8,9},{9,8},{10,11... | collective-permute-start | bytes 3538952 | tf_op jit(solution)/shard_map/ppermute | solution.py:25
  126.9 30.8 %collective-permute-start.17 = (bf16[768,768]{1,0:T(8,128)(2,1)S(1)}, bf16[768,768]{1,0:T(8,128)(2,1)S(1)}, u32[]{:S(2)}, u32[]{:S(2)}) collective-permute-start(bf16[768,768]{1,0:T(8,128)(2,1)S(1)} %constant_dynamic-slice_fusion.21), channel_id=1, source_target_pairs={{0,4},{12,8},{1,5},{13,9},{2,6},{14,10},{3,7},{15,11},{16,20},{28,... | collective-permute-start | bytes 3538952 | tf_op jit(solution)/shard_map/ppermute | solution.py:77
  134.3 20.3 %collective-permute-start.12 = (bf16[512,768]{1,0:T(8,128)(2,1)S(1)}, bf16[512,768]{1,0:T(8,128)(2,1)S(1)}, u32[]{:S(2)}, u32[]{:S(2)}) collective-permute-start(bf16[512,768]{1,0:T(8,128)(2,1)S(1)} %constant_dynamic-slice_fusion.19), channel_id=1, source_target_pairs={{4,8},{8,4},{5,9},{9,5},{6,10},{10,6},{7,11},{11,7},{20,24},{24,20... | collective-permute-start | bytes 2359304 | tf_op jit(solution)/shard_map/ppermute | solution.py:104
  138.2 34.2 %collective-permute-start.39 = (bf16[768,768]{1,0:T(8,128)(2,1)S(1)}, bf16[768,768]{1,0:T(8,128)(2,1)S(1)}, u32[]{:S(2)}, u32[]{:S(2)}) collective-permute-start(bf16[768,768]{1,0:T(8,128)(2,1)S(1)} %copy-done.50), channel_id=1, source_target_pairs={{0,1},{1,0},{2,3},{3,2},{4,5},{5,4},{6,7},{7,6},{8,9},{9,8},{10,11... | collective-permute-start | bytes 3538952 | tf_op jit(solution)/shard_map/ppermute | solution.py:25
  158.6 39.7 %collective-permute-start.18 = (bf16[768,768]{1,0:T(8,128)(2,1)S(1)}, bf16[768,768]{1,0:T(8,128)(2,1)S(1)}, u32[]{:S(2)}, u32[]{:S(2)}) collective-permute-start(bf16[768,768]{1,0:T(8,128)(2,1)S(1)} %constant_dynamic-slice_fusion.18), channel_id=1, source_target_pairs={{0,4},{12,8},{1,5},{13,9},{2,6},{14,10},{3,7},{15,11},{16,20},{28,... | collective-permute-start | bytes 3538952 | tf_op jit(solution)/shard_map/ppermute | solution.py:77
  166.3 30.6 %collective-permute-start.20 = (bf16[512,768]{1,0:T(8,128)(2,1)S(1)}, bf16[512,768]{1,0:T(8,128)(2,1)S(1)}, u32[]{:S(2)}, u32[]{:S(2)}) collective-permute-start(bf16[512,768]{1,0:T(8,128)(2,1)S(1)} %constant_dynamic-slice_fusion.14), channel_id=1, source_target_pairs={{4,8},{8,4},{5,9},{9,5},{6,10},{10,6},{7,11},{11,7},{20,24},{24,20... | collective-permute-start | bytes 2359304 | tf_op jit(solution)/shard_map/ppermute | solution.py:104
  169.8 24.3 %collective-permute-start.23 = (bf16[256,768]{1,0:T(8,128)(2,1)S(1)}, bf16[256,768]{1,0:T(8,128)(2,1)S(1)}, u32[]{:S(2)}, u32[]{:S(2)}) collective-permute-start(bf16[256,768]{1,0:T(8,128)(2,1)S(1)} %add_convert_fusion.21), channel_id=1, source_target_pairs={{8,12},{4,0},{9,13},{5,1},{10,14},{6,2},{11,15},{7,3},{24,28},{20,... | collective-permute-start | bytes 1179656 | tf_op jit(solution)/shard_map/ppermute | solution.py:77
  174.5 44.9 %collective-permute-start.16 = (bf16[768,768]{1,0:T(8,128)(2,1)S(1)}, bf16[768,768]{1,0:T(8,128)(2,1)S(1)}, u32[]{:S(2)}, u32[]{:S(2)}) collective-permute-start(bf16[768,768]{1,0:T(8,128)(2,1)S(1)} %constant_dynamic-slice_fusion.17), channel_id=1, source_target_pairs={{8,12},{4,0},{9,13},{5,1},{10,14},{6,2},{11,15},{7,3},{24,28},{20,... | collective-permute-start | bytes 3538952 | tf_op jit(solution)/shard_map/ppermute | solution.py:104
  199.2 74.7 %collective-permute-start.27 = (bf16[768,768]{1,0:T(8,128)(2,1)}, bf16[768,768]{1,0:T(8,128)(2,1)}, u32[]{:S(2)}, u32[]{:S(2)}) collective-permute-start(bf16[768,768]{1,0:T(8,128)(2,1)} %constant_dynamic-slice_fusion.12), channel_id=1, source_target_pairs={{8,12},{4,0},{9,13},{5,1},{10,14},{6,2},{11,15},{7,3},{24,28},{20,... | collective-permute-start | bytes 3538952 | tf_op jit(solution)/shard_map/ppermute | solution.py:104
  200.5 46.3 %collective-permute-start.28 = (bf16[768,768]{1,0:T(8,128)(2,1)S(1)}, bf16[768,768]{1,0:T(8,128)(2,1)S(1)}, u32[]{:S(2)}, u32[]{:S(2)}) collective-permute-start(bf16[768,768]{1,0:T(8,128)(2,1)S(1)} %constant_dynamic-slice_fusion.13), channel_id=1, source_target_pairs={{0,4},{12,8},{1,5},{13,9},{2,6},{14,10},{3,7},{15,11},{16,20},{28,... | collective-permute-start | bytes 3538952 | tf_op jit(solution)/shard_map/ppermute | solution.py:77
  206.4 39.0 %collective-permute-start.29 = (bf16[512,768]{1,0:T(8,128)(2,1)S(1)}, bf16[512,768]{1,0:T(8,128)(2,1)S(1)}, u32[]{:S(2)}, u32[]{:S(2)}) collective-permute-start(bf16[512,768]{1,0:T(8,128)(2,1)S(1)} %constant_dynamic-slice_fusion.11), channel_id=1, source_target_pairs={{4,8},{8,4},{5,9},{9,5},{6,10},{10,6},{7,11},{11,7},{20,24},{24,20... | collective-permute-start | bytes 2359304 | tf_op jit(solution)/shard_map/ppermute | solution.py:104
  211.0 31.8 %collective-permute-start.30 = (bf16[256,768]{1,0:T(8,128)(2,1)S(1)}, bf16[256,768]{1,0:T(8,128)(2,1)S(1)}, u32[]{:S(2)}, u32[]{:S(2)}) collective-permute-start(bf16[256,768]{1,0:T(8,128)(2,1)S(1)} %add_convert_fusion.20), channel_id=1, source_target_pairs={{8,12},{4,0},{9,13},{5,1},{10,14},{6,2},{11,15},{7,3},{24,28},{20,... | collective-permute-start | bytes 1179656 | tf_op jit(solution)/shard_map/ppermute | solution.py:77
  223.5 41.8 %collective-permute-start.62 = (bf16[768,768]{1,0:T(8,128)(2,1)S(1)}, bf16[768,768]{1,0:T(8,128)(2,1)S(1)}, u32[]{:S(2)}, u32[]{:S(2)}) collective-permute-start(bf16[768,768]{1,0:T(8,128)(2,1)S(1)} %slice.749), channel_id=1, source_target_pairs={{0,1},{1,0},{2,3},{3,2},{4,5},{5,4},{6,7},{7,6},{8,9},{9,8},{10,11... | collective-permute-start | bytes 3538952 | tf_op jit(solution)/shard_map/ppermute | solution.py:25
  247.0 24.3 %collective-permute-start.31 = (bf16[512,768]{1,0:T(8,128)(2,1)S(1)}, bf16[512,768]{1,0:T(8,128)(2,1)S(1)}, u32[]{:S(2)}, u32[]{:S(2)}) collective-permute-start(bf16[512,768]{1,0:T(8,128)(2,1)S(1)} %add_convert_fusion.11), channel_id=1, source_target_pairs={{4,8},{8,4},{5,9},{9,5},{6,10},{10,6},{7,11},{11,7},{20,24},{24,20... | collective-permute-start | bytes 2359304 | tf_op jit(solution)/shard_map/ppermute | solution.py:77
  247.8 74.4 %collective-permute-start.34 = (bf16[768,768]{1,0:T(8,128)(2,1)}, bf16[768,768]{1,0:T(8,128)(2,1)}, u32[]{:S(2)}, u32[]{:S(2)}) collective-permute-start(bf16[768,768]{1,0:T(8,128)(2,1)} %constant_dynamic-slice_fusion.9), channel_id=1, source_target_pairs={{8,12},{4,0},{9,13},{5,1},{10,14},{6,2},{11,15},{7,3},{24,28},{20,... | collective-permute-start | bytes 3538952 | tf_op jit(solution)/shard_map/ppermute | solution.py:104
  255.0 40.3 %collective-permute-start.35 = (bf16[768,768]{1,0:T(8,128)(2,1)}, bf16[768,768]{1,0:T(8,128)(2,1)}, u32[]{:S(2)}, u32[]{:S(2)}) collective-permute-start(bf16[768,768]{1,0:T(8,128)(2,1)} %constant_dynamic-slice_fusion.10), channel_id=1, source_target_pairs={{0,4},{12,8},{1,5},{13,9},{2,6},{14,10},{3,7},{15,11},{16,20},{28,... | collective-permute-start | bytes 3538952 | tf_op jit(solution)/shard_map/ppermute | solution.py:77
  265.2 28.6 %collective-permute-start.36 = (bf16[512,768]{1,0:T(8,128)(2,1)}, bf16[512,768]{1,0:T(8,128)(2,1)}, u32[]{:S(2)}, u32[]{:S(2)}) collective-permute-start(bf16[512,768]{1,0:T(8,128)(2,1)} %constant_dynamic-slice_fusion.8), channel_id=1, source_target_pairs={{4,8},{8,4},{5,9},{9,5},{6,10},{10,6},{7,11},{11,7},{20,24},{24,20... | collective-permute-start | bytes 2359304 | tf_op jit(solution)/shard_map/ppermute | solution.py:104
  280.0 33.1 %collective-permute-start.63 = (bf16[768,768]{1,0:T(8,128)(2,1)}, bf16[768,768]{1,0:T(8,128)(2,1)}, u32[]{:S(2)}, u32[]{:S(2)}) collective-permute-start(bf16[768,768]{1,0:T(8,128)(2,1)} %slice.751), channel_id=1, source_target_pairs={{0,1},{1,0},{2,3},{3,2},{4,5},{5,4},{6,7},{7,6},{8,9},{9,8},{10,11... | collective-permute-start | bytes 3538952 | tf_op jit(solution)/shard_map/ppermute | solution.py:25
  296.7 21.6 %collective-permute-start.38 = (bf16[512,768]{1,0:T(8,128)(2,1)S(1)}, bf16[512,768]{1,0:T(8,128)(2,1)S(1)}, u32[]{:S(2)}, u32[]{:S(2)}) collective-permute-start(bf16[512,768]{1,0:T(8,128)(2,1)S(1)} %add_convert_fusion.10), channel_id=1, source_target_pairs={{4,8},{8,4},{5,9},{9,5},{6,10},{10,6},{7,11},{11,7},{20,24},{24,20... | collective-permute-start | bytes 2359304 | tf_op jit(solution)/shard_map/ppermute | solution.py:77
  297.6 67.5 %collective-permute-start.41 = (bf16[768,768]{1,0:T(8,128)(2,1)}, bf16[768,768]{1,0:T(8,128)(2,1)}, u32[]{:S(2)}, u32[]{:S(2)}) collective-permute-start(bf16[768,768]{1,0:T(8,128)(2,1)} %constant_dynamic-slice_fusion.6), channel_id=1, source_target_pairs={{8,12},{4,0},{9,13},{5,1},{10,14},{6,2},{11,15},{7,3},{24,28},{20,... | collective-permute-start | bytes 3538952 | tf_op jit(solution)/shard_map/ppermute | solution.py:104
  302.8 40.6 %collective-permute-start.42 = (bf16[768,768]{1,0:T(8,128)(2,1)}, bf16[768,768]{1,0:T(8,128)(2,1)}, u32[]{:S(2)}, u32[]{:S(2)}) collective-permute-start(bf16[768,768]{1,0:T(8,128)(2,1)} %constant_dynamic-slice_fusion.7), channel_id=1, source_target_pairs={{0,4},{12,8},{1,5},{13,9},{2,6},{14,10},{3,7},{15,11},{16,20},{28,... | collective-permute-start | bytes 3538952 | tf_op jit(solution)/shard_map/ppermute | solution.py:77
  313.1 28.9 %collective-permute-start.43 = (bf16[512,768]{1,0:T(8,128)(2,1)}, bf16[512,768]{1,0:T(8,128)(2,1)}, u32[]{:S(2)}, u32[]{:S(2)}) collective-permute-start(bf16[512,768]{1,0:T(8,128)(2,1)} %constant_dynamic-slice_fusion.5), channel_id=1, source_target_pairs={{4,8},{8,4},{5,9},{9,5},{6,10},{10,6},{7,11},{11,7},{20,24},{24,20... | collective-permute-start | bytes 2359304 | tf_op jit(solution)/shard_map/ppermute | solution.py:104
  328.3 29.1 %collective-permute-start.64 = (bf16[768,768]{1,0:T(8,128)(2,1)}, bf16[768,768]{1,0:T(8,128)(2,1)}, u32[]{:S(2)}, u32[]{:S(2)}) collective-permute-start(bf16[768,768]{1,0:T(8,128)(2,1)} %slice.755), channel_id=1, source_target_pairs={{0,1},{1,0},{2,3},{3,2},{4,5},{5,4},{6,7},{7,6},{8,9},{9,8},{10,11... | collective-permute-start | bytes 3538952 | tf_op jit(solution)/shard_map/ppermute | solution.py:25
  345.5 59.7 %collective-permute-start.47 = (bf16[768,768]{1,0:T(8,128)(2,1)}, bf16[768,768]{1,0:T(8,128)(2,1)}, u32[]{:S(2)}, u32[]{:S(2)}) collective-permute-start(bf16[768,768]{1,0:T(8,128)(2,1)} %constant_dynamic-slice_fusion.2), channel_id=1, source_target_pairs={{8,12},{4,0},{9,13},{5,1},{10,14},{6,2},{11,15},{7,3},{24,28},{20,... | collective-permute-start | bytes 3538952 | tf_op jit(solution)/shard_map/ppermute | solution.py:104
  351.0 40.8 %collective-permute-start.48 = (bf16[768,768]{1,0:T(8,128)(2,1)}, bf16[768,768]{1,0:T(8,128)(2,1)}, u32[]{:S(2)}, u32[]{:S(2)}) collective-permute-start(bf16[768,768]{1,0:T(8,128)(2,1)} %constant_dynamic-slice_fusion.4), channel_id=1, source_target_pairs={{0,4},{12,8},{1,5},{13,9},{2,6},{14,10},{3,7},{15,11},{16,20},{28,... | collective-permute-start | bytes 3538952 | tf_op jit(solution)/shard_map/ppermute | solution.py:77
  357.5 31.7 %collective-permute-start.49 = (bf16[512,768]{1,0:T(8,128)(2,1)}, bf16[512,768]{1,0:T(8,128)(2,1)}, u32[]{:S(2)}, u32[]{:S(2)}) collective-permute-start(bf16[512,768]{1,0:T(8,128)(2,1)} %constant_dynamic-slice_fusion.1), channel_id=1, source_target_pairs={{4,8},{8,4},{5,9},{9,5},{6,10},{10,6},{7,11},{11,7},{20,24},{24,20... | collective-permute-start | bytes 2359304 | tf_op jit(solution)/shard_map/ppermute | solution.py:104
  363.6 21.5 %collective-permute-start.50 = (bf16[256,768]{1,0:T(8,128)(2,1)}, bf16[256,768]{1,0:T(8,128)(2,1)}, u32[]{:S(2)}, u32[]{:S(2)}) collective-permute-start(bf16[256,768]{1,0:T(8,128)(2,1)} %add_convert_fusion.17), channel_id=1, source_target_pairs={{8,12},{4,0},{9,13},{5,1},{10,14},{6,2},{11,15},{7,3},{24,28},{20,... | collective-permute-start | bytes 1179656 | tf_op jit(solution)/shard_map/ppermute | solution.py:77
  371.2 28.7 %collective-permute-start.65 = (bf16[768,768]{1,0:T(8,128)(2,1)}, bf16[768,768]{1,0:T(8,128)(2,1)}, u32[]{:S(2)}, u32[]{:S(2)}) collective-permute-start(bf16[768,768]{1,0:T(8,128)(2,1)} %slice.759), channel_id=1, source_target_pairs={{0,1},{1,0},{2,3},{3,2},{4,5},{5,4},{6,7},{7,6},{8,9},{9,8},{10,11... | collective-permute-start | bytes 3538952 | tf_op jit(solution)/shard_map/ppermute | solution.py:25
  390.5 58.2 %collective-permute-start.53 = (bf16[768,768]{1,0:T(8,128)(2,1)}, bf16[768,768]{1,0:T(8,128)(2,1)}, u32[]{:S(2)}, u32[]{:S(2)}) collective-permute-start(bf16[768,768]{1,0:T(8,128)(2,1)} %constant_dynamic-slice_fusion), channel_id=1, source_target_pairs={{8,12},{4,0},{9,13},{5,1},{10,14},{6,2},{11,15},{7,3},{24,28},{20,... | collective-permute-start | bytes 3538952 | tf_op jit(solution)/shard_map/ppermute | solution.py:104
  398.4 39.8 %collective-permute-start.56 = (bf16[512,768]{1,0:T(8,128)(2,1)}, bf16[512,768]{1,0:T(8,128)(2,1)}, u32[]{:S(2)}, u32[]{:S(2)}) collective-permute-start(bf16[512,768]{1,0:T(8,128)(2,1)} %constant_dynamic-slice_fusion.16), channel_id=1, source_target_pairs={{4,8},{8,4},{5,9},{9,5},{6,10},{10,6},{7,11},{11,7},{20,24},{24,20... | collective-permute-start | bytes 2359304 | tf_op jit(solution)/shard_map/ppermute | solution.py:104
  403.6 25.0 %collective-permute-start.54 = (bf16[256,768]{1,0:T(8,128)(2,1)S(1)}, bf16[256,768]{1,0:T(8,128)(2,1)}, u32[]{:S(2)}, u32[]{:S(2)}) collective-permute-start(bf16[256,768]{1,0:T(8,128)(2,1)S(1)} %add_convert_fusion.16), channel_id=1, source_target_pairs={{8,12},{4,0},{9,13},{5,1},{10,14},{6,2},{11,15},{7,3},{24,28},{20,... | collective-permute-start | bytes 1179656 | tf_op jit(solution)/shard_map/ppermute | solution.py:77
  411.3 49.8 %collective-permute-start.66 = (bf16[768,768]{1,0:T(8,128)(2,1)}, bf16[768,768]{1,0:T(8,128)(2,1)}, u32[]{:S(2)}, u32[]{:S(2)}) collective-permute-start(bf16[768,768]{1,0:T(8,128)(2,1)} %slice.763), channel_id=1, source_target_pairs={{0,1},{1,0},{2,3},{3,2},{4,5},{5,4},{6,7},{7,6},{8,9},{9,8},{10,11... | collective-permute-start | bytes 3538952 | tf_op jit(solution)/shard_map/ppermute | solution.py:25
  439.6 29.7 %collective-permute-start.57 = (bf16[768,768]{1,0:T(8,128)(2,1)}, bf16[768,768]{1,0:T(8,128)(2,1)}, u32[]{:S(2)}, u32[]{:S(2)}) collective-permute-start(bf16[768,768]{1,0:T(8,128)(2,1)} %constant_dynamic-slice_fusion.3), channel_id=1, source_target_pairs={{8,12},{4,0},{9,13},{5,1},{10,14},{6,2},{11,15},{7,3},{24,28},{20,... | collective-permute-start | bytes 3538952 | tf_op jit(solution)/shard_map/ppermute | solution.py:104
  454.8 27.1 %collective-permute-start.67 = (bf16[768,768]{1,0:T(8,128)(2,1)}, bf16[768,768]{1,0:T(8,128)(2,1)S(1)}, u32[]{:S(2)}, u32[]{:S(2)}) collective-permute-start(bf16[768,768]{1,0:T(8,128)(2,1)} %slice.767), channel_id=1, source_target_pairs={{0,1},{1,0},{2,3},{3,2},{4,5},{5,4},{6,7},{7,6},{8,9},{9,8},{10,11... | collective-permute-start | bytes 3538952 | tf_op jit(solution)/shard_map/ppermute | solution.py:25
  465.1 32.5 %collective-permute-start.59 = (bf16[768,768]{1,0:T(8,128)(2,1)S(1)}, bf16[768,768]{1,0:T(8,128)(2,1)}, u32[]{:S(2)}, u32[]{:S(2)}) collective-permute-start(bf16[768,768]{1,0:T(8,128)(2,1)S(1)} %constant_dynamic-slice_fusion.15), channel_id=1, source_target_pairs={{8,12},{4,0},{9,13},{5,1},{10,14},{6,2},{11,15},{7,3},{24,28},{20,... | collective-permute-start | bytes 3538952 | tf_op jit(solution)/shard_map/ppermute | solution.py:104
  475.5 40.2 %collective-permute-start.68 = (bf16[768,768]{1,0:T(8,128)(2,1)}, bf16[768,768]{1,0:T(8,128)(2,1)}, u32[]{:S(2)}, u32[]{:S(2)}) collective-permute-start(bf16[768,768]{1,0:T(8,128)(2,1)} %slice.771), channel_id=1, source_target_pairs={{0,1},{1,0},{2,3},{3,2},{4,5},{5,4},{6,7},{7,6},{8,9},{9,8},{10,11... | collective-permute-start | bytes 3538952 | tf_op jit(solution)/shard_map/ppermute | solution.py:25
  504.3 19.0 %collective-permute-start.69 = (bf16[768,768]{1,0:T(8,128)(2,1)}, bf16[768,768]{1,0:T(8,128)(2,1)}, u32[]{:S(2)}, u32[]{:S(2)}) collective-permute-start(bf16[768,768]{1,0:T(8,128)(2,1)} %slice.775), channel_id=1, source_target_pairs={{0,1},{1,0},{2,3},{3,2},{4,5},{5,4},{6,7},{7,6},{8,9},{9,8},{10,11... | collective-permute-start | bytes 3538952 | tf_op jit(solution)/shard_map/ppermute | solution.py:25
  521.9 18.7 %collective-permute-start.61 = (bf16[256,1536]{1,0:T(8,128)(2,1)S(1)}, bf16[256,1536]{1,0:T(8,128)(2,1)S(1)}, u32[]{:S(2)}, u32[]{:S(2)}) collective-permute-start(bf16[256,1536]{1,0:T(8,128)(2,1)S(1)} %select_convert_fusion.1), channel_id=1, source_target_pairs={{0,2},{2,0},{1,3},{3,1},{4,6},{6,4},{5,7},{7,5},{8,10},{10,8},{9,1... | collective-permute-start | bytes 2359304 | tf_op jit(solution)/shard_map/ppermute | solution.py:25
  (84 other events, 772.0 us)

commit v3 on v2

--- a/solution.py
+++ b/solution.py
@@ -192,10 +192,11 @@
         lines[c].gather_place(steps - 1)
         grad = lines[c].whole
         bias_sums.append(jnp.sum(grad, axis=0, dtype=F32))
-        w_grad = lax.dot_general(tokens, grad, (((0,), (0,)), ((), ())), preferred_element_type=F32).astype(BF16)
-        w_own, w_other = w_grad[:mine], swap(w_grad[mine:], "gz")
         term = lax.dot_general(grad, weights[c], (((1,), (1,)), ((), ())), preferred_element_type=F32)
         input_sum = (input_sum.astype(F32) + term).astype(BF16)
+        w_rows = after(grad, input_sum) if c + 1 == count else grad
+        w_grad = lax.dot_general(tokens, w_rows, (((0,), (0,)), ((), ())), preferred_element_type=F32).astype(BF16)
+        w_own, w_other = w_grad[:mine], swap(w_grad[mine:], "gz")
         note(w_grad, input_sum)
         weight_grad = weight_grad.at[:, start : start + width].set(by_core(core, w_own, w_other))
         weight_grad = weight_grad.at[:, half + start : half + start + width].set(by_core(core, w_other, w_own))

time: 553 us -> 556 us (level)
    unnamed x129 -> x131, local copies, waits for them, and re-layouts: 12.7 us -> 12.3 us
where the time goes in v3:
time: 556 us; the launch traced here: 546 us
  waiting for transfers between devices  163 us (29%)
  starting transfers between devices  126 us (23%)
  other arithmetic  118 us (21%)
  matrix products  95.3 us (17%)
  local copies, waits for them, and re-layouts  40.1 us (7%)
    ppermute x24, waiting for transfers between devices, reduce_permute(): lax.ppermute(send, 'gx', [(s, s + 1), (n - 1 - s, n - 2 - s)])  94.1 us
    ppermute x24, starting transfers between devices, reduce_permute(): lax.ppermute(send, 'gx', [(s, s + 1), (n - 1 - s, n - 2 - s)])  77.6 us
    ppermute x24, waiting for transfers between devices, gather_permute(): lax.ppermute(send, 'gx', [(u, u + 1), (n - 1 - u, n - 2 - u)])  51.3 us
    dot_general x8, matrix products, use(): lax.dot_general(grad, weights[c], (((1,), (1,)), ((), ())), preferred_ele...  46.3 us
    ppermute x24, starting transfers between devices, gather_permute(): lax.ppermute(send, 'gx', [(u, u + 1), (n - 1 - u, n - 2 - u)])  42.2 us
    dot_general x8, matrix products, use(): lax.dot_general(tokens, w_rows, (((0,), (0,)), ((), ())), preferred_eleme...  26.9 us
    select_n x9, other arithmetic, by_core(): return jnp.where(core == 0, first, second)  23.2 us
    dot_general x8, matrix products, multiply(): jnp.dot(tokens, ordered(w), preferred_element_type=F32).astype(BF16)  22.1 us
  transfers between devices with their start and end apart: 71, of which 23 were waited for; matrix products, arithmetic and copies ran while one was open for 44% of the time, Pallas kernels for 0%

profile of v3, /device:TPU:0, one launch (start us, length us, event | category | flops | bytes accessed | tf_op | source)
XLA Modules:
  0.0 545.6 jit_solution(11553006452769053854)
XLA Ops:
  3.6 6.9 %broadcast_select_fusion.8 = (bf16[768,768]{1,0:T(8,128)(2,1)}, bf16[768,768]{1,0:T(8,128)(2,1)}, bf16[768,768]{1,0:T(8,128)(2,1)}, bf16[768,768]{1,0:T(8,128)(2...) fusion(pred[]{:T(512)S(6)} %eq.13, bf16[768,12288]{1,0:T(8,128)(2,1)} %param.37), kind=kLoop, calls=%fused_computation.135 | loop fusion | flops 4128768 | bytes 17694720 | tf_op jit(solution)/shard_map/jit(_where)/select_n | solution.py:21
  11.1 8.8 %broadcast_select_fusion.9 = (bf16[768,768]{1,0:T(8,128)(2,1)}, bf16[768,768]{1,0:T(8,128)(2,1)}, bf16[768,768]{1,0:T(8,128)(2,1)}, bf16[768,768]{1,0:T(8,128)(2...) fusion(pred[]{:T(512)S(6)} %eq.13, ...), kind=kLoop, calls=%fused_computation.136 | loop fusion | flops 5308416 | bytes 22413312 | tf_op jit(solution)/shard_map/jit(_where)/select_n | solution.py:21
  30.0 3.9 convolution_convert_fusion.16
  36.1 4.5 collective-permute-start.5
  56.6 9.1 %collective-permute-done.5 = bf16[768,768]{1,0:T(8,128)(2,1)} collective-permute-done((bf16[768,768]{1,0:T(8,128)(2,1)}, bf16[768,768]{1,0:T(8,128)(2,1)}, u32[]{:S(2)}, u32[]{:S(2)}) %collective-permute-start.5) | collective-permute-done | bytes 1179680 | tf_op jit(solution)/shard_map/ppermute | solution.py:77
  71.9 21.4 %collective-permute-start.11 = (bf16[768,768]{1,0:T(8,128)(2,1)S(1)}, bf16[768,768]{1,0:T(8,128)(2,1)S(1)}, u32[]{:S(2)}, u32[]{:S(2)}) collective-permute-start(bf16[768,768]{1,0:T(8,128)(2,1)S(1)} %constant_dynamic-slice_fusion.22), channel_id=1, source_target_pairs={{0,4},{12,8},{1,5},{13,9},{2,6},{14,10},{3,7},{15,11},{16,20},{28,... | collective-permute-start | bytes 3538952 | tf_op jit(solution)/shard_map/ppermute | solution.py:77
  97.0 8.9 %collective-permute-done.9 = bf16[256,768]{1,0:T(8,128)(2,1)S(1)} collective-permute-done((bf16[256,768]{1,0:T(8,128)(2,1)S(1)}, bf16[256,768]{1,0:T(8,128)(2,1)S(1)}, u32[]{:S(2)}, u32[]{:S(2)}) %collective-permute-start.9) | collective-permute-done | bytes 393248 | tf_op jit(solution)/shard_map/ppermute | solution.py:77
  111.2 8.4 %collective-permute-done.11 = bf16[768,768]{1,0:T(8,128)(2,1)S(1)} collective-permute-done((bf16[768,768]{1,0:T(8,128)(2,1)S(1)}, bf16[768,768]{1,0:T(8,128)(2,1)S(1)}, u32[]{:S(2)}, u32[]{:S(2)}) %collective-permute-start.11) | collective-permute-done | bytes 1179680 | tf_op jit(solution)/shard_map/ppermute | solution.py:77
  120.5 6.2 %collective-permute-done.10 = bf16[256,768]{1,0:T(8,128)(2,1)S(1)} collective-permute-done((bf16[256,768]{1,0:T(8,128)(2,1)S(1)}, bf16[256,768]{1,0:T(8,128)(2,1)S(1)}, u32[]{:S(2)}, u32[]{:S(2)}) %collective-permute-start.10) | collective-permute-done | bytes 393248 | tf_op jit(solution)/shard_map/ppermute | solution.py:104
  126.8 4.4 collective-permute-start.17
  138.7 13.1 %collective-permute-done.15 = bf16[256,768]{1,0:T(8,128)(2,1)S(1)} collective-permute-done((bf16[256,768]{1,0:T(8,128)(2,1)S(1)}, bf16[256,768]{1,0:T(8,128)(2,1)S(1)}, u32[]{:S(2)}, u32[]{:S(2)}) %collective-permute-start.15) | collective-permute-done | bytes 393248 | tf_op jit(solution)/shard_map/ppermute | solution.py:77
  158.5 7.2 %collective-permute-start.18 = (bf16[768,768]{1,0:T(8,128)(2,1)S(1)}, bf16[768,768]{1,0:T(8,128)(2,1)S(1)}, u32[]{:S(2)}, u32[]{:S(2)}) collective-permute-start(bf16[768,768]{1,0:T(8,128)(2,1)S(1)} %constant_dynamic-slice_fusion.18), channel_id=1, source_target_pairs={{0,4},{12,8},{1,5},{13,9},{2,6},{14,10},{3,7},{15,11},{16,20},{28,... | collective-permute-start | bytes 3538952 | tf_op jit(solution)/shard_map/ppermute | solution.py:77
  175.7 18.3 %collective-permute-done.23 = bf16[256,768]{1,0:T(8,128)(2,1)S(1)} collective-permute-done((bf16[256,768]{1,0:T(8,128)(2,1)S(1)}, bf16[256,768]{1,0:T(8,128)(2,1)S(1)}, u32[]{:S(2)}, u32[]{:S(2)}) %collective-permute-start.23) | collective-permute-done | bytes 393248 | tf_op jit(solution)/shard_map/ppermute | solution.py:77
  200.4 5.7 %collective-permute-start.28 = (bf16[768,768]{1,0:T(8,128)(2,1)S(1)}, bf16[768,768]{1,0:T(8,128)(2,1)S(1)}, u32[]{:S(2)}, u32[]{:S(2)}) collective-permute-start(bf16[768,768]{1,0:T(8,128)(2,1)S(1)} %constant_dynamic-slice_fusion.13), channel_id=1, source_target_pairs={{0,4},{12,8},{1,5},{13,9},{2,6},{14,10},{3,7},{15,11},{16,20},{28,... | collective-permute-start | bytes 3538952 | tf_op jit(solution)/shard_map/ppermute | solution.py:77
  212.2 7.1 %collective-permute-done.16 = bf16[768,768]{1,0:T(8,128)(2,1)S(1)} collective-permute-done((bf16[768,768]{1,0:T(8,128)(2,1)S(1)}, bf16[768,768]{1,0:T(8,128)(2,1)S(1)}, u32[]{:S(2)}, u32[]{:S(2)}) %collective-permute-start.16) | collective-permute-done | bytes 1179680 | tf_op jit(solution)/shard_map/ppermute | solution.py:104
  219.7 3.3 convolution_convert_fusion.8
  224.5 5.3 convolution_convert_fusion
  229.8 12.9 %collective-permute-done.30 = bf16[256,768]{1,0:T(8,128)(2,1)S(1)} collective-permute-done((bf16[256,768]{1,0:T(8,128)(2,1)S(1)}, bf16[256,768]{1,0:T(8,128)(2,1)S(1)}, u32[]{:S(2)}, u32[]{:S(2)}) %collective-permute-start.30) | collective-permute-done | bytes 393248 | tf_op jit(solution)/shard_map/ppermute | solution.py:77
  249.0 5.9 %collective-permute-done.33 = bf16[256,768]{1,0:T(8,128)(2,1)S(1)} collective-permute-done((bf16[256,768]{1,0:T(8,128)(2,1)S(1)}, bf16[256,768]{1,0:T(8,128)(2,1)S(1)}, u32[]{:S(2)}, u32[]{:S(2)}) %collective-permute-start.33) | collective-permute-done | bytes 393248 | tf_op jit(solution)/shard_map/ppermute | solution.py:104
  254.9 5.4 collective-permute-start.35
  275.6 3.3 convolution_convert_fusion.7
  280.0 6.1 %add_convert_fusion.6 = bf16[1024,1536]{1,0:T(8,128)(2,1)} fusion(bf16[1024,1536]{1,0:T(8,128)(2,1)} %convolution_convert_fusion, bf16[1024,768]{1,0:T(8,128)(2,1)S(1)} %select_dynamic-update-slice_fusion.8, bf16[768,768]{1,0:T(8,128)(2,1)} %collective-permute-done.6, bf16[768,768]{1,0:T(8,128)(2,1)} %get-tuple-element.340), kind=kOutput, calls=%fused_computation.7 | convolution fusion | flops 2425356288 | bytes 10223616 | tf_op jit(solution)/shard_map/dot_general | solution.py:195
  289.7 4.0 collective-permute-start.40
  298.8 3.9 collective-permute-done.40
  302.8 5.4 collective-permute-start.42
  323.8 3.3 convolution_convert_fusion.6
  328.2 6.1 %add_convert_fusion.5 = bf16[1024,1536]{1,0:T(8,128)(2,1)} fusion(bf16[1024,1536]{1,0:T(8,128)(2,1)} %add_convert_fusion.6, bf16[1024,768]{1,0:T(8,128)(2,1)S(1)} %select_dynamic-update-slice_fusion.7, bf16[768,768]{1,0:T(8,128)(2,1)} %collective-permute-done.8, bf16[768,768]{1,0:T(8,128)(2,1)} %get-tuple-element.342), kind=kOutput, calls=%fused_computation.6 | convolution fusion | flops 2425356288 | bytes 10223616 | tf_op jit(solution)/shard_map/dot_general | solution.py:195
  346.6 4.2 collective-permute-done.46
  350.9 5.4 collective-permute-start.48
  366.8 3.3 convolution_convert_fusion.5
  371.2 6.1 %add_convert_fusion.4 = bf16[1024,1536]{1,0:T(8,128)(2,1)} fusion(bf16[1024,1536]{1,0:T(8,128)(2,1)} %add_convert_fusion.5, bf16[1024,768]{1,0:T(8,128)(2,1)S(1)} %select_dynamic-update-slice_fusion.6, bf16[768,768]{1,0:T(8,128)(2,1)} %collective-permute-done.14, bf16[768,768]{1,0:T(8,128)(2,1)} %get-tuple-element.344), kind=kOutput, calls=%fused_computation.5 | convolution fusion | flops 2425356288 | bytes 10223616 | tf_op jit(solution)/shard_map/dot_general | solution.py:195
  377.6 7.4 %collective-permute-done.50 = bf16[256,768]{1,0:T(8,128)(2,1)} collective-permute-done((bf16[256,768]{1,0:T(8,128)(2,1)}, bf16[256,768]{1,0:T(8,128)(2,1)}, u32[]{:S(2)}, u32[]{:S(2)}) %collective-permute-start.50) | collective-permute-done | bytes 393248 | tf_op jit(solution)/shard_map/ppermute | solution.py:77
  393.8 3.4 collective-permute-done.52
  406.8 3.3 convolution_convert_fusion.4
  411.8 5.8 %add_convert_fusion.3 = bf16[1024,1536]{1,0:T(8,128)(2,1)} fusion(bf16[1024,1536]{1,0:T(8,128)(2,1)} %add_convert_fusion.4, bf16[1024,768]{1,0:T(8,128)(2,1)S(1)} %select_dynamic-update-slice_fusion.5, bf16[768,768]{1,0:T(8,128)(2,1)} %copy-done.59, bf16[768,768]{1,0:T(8,128)(2,1)S(1)} %copy-done.16), kind=kOutput, calls=%fused_computation.4 | convolution fusion | flops 2425356288 | bytes 10223616 | tf_op jit(solution)/shard_map/dot_general | solution.py:195
  417.8 10.6 %collective-permute-done.54 = bf16[256,768]{1,0:T(8,128)(2,1)} collective-permute-done((bf16[256,768]{1,0:T(8,128)(2,1)S(1)}, bf16[256,768]{1,0:T(8,128)(2,1)}, u32[]{:S(2)}, u32[]{:S(2)}) %collective-permute-start.54) | collective-permute-done | bytes 393248 | tf_op jit(solution)/shard_map/ppermute | solution.py:77
  430.9 7.2 %collective-permute-start.55 = (bf16[256,768]{1,0:T(8,128)(2,1)S(1)}, bf16[256,768]{1,0:T(8,128)(2,1)S(1)}, u32[]{:S(2)}, u32[]{:S(2)}) collective-permute-start(bf16[256,768]{1,0:T(8,128)(2,1)S(1)} %get-tuple-element.324), channel_id=1, source_target_pairs={{0,4},{12,8},{1,5},{13,9},{2,6},{14,10},{3,7},{15,11},{16,20},{28,... | collective-permute-start | bytes 1179656 | tf_op jit(solution)/shard_map/ppermute | solution.py:104
  440.8 5.7 %collective-permute-done.55 = bf16[256,768]{1,0:T(8,128)(2,1)S(1)} collective-permute-done((bf16[256,768]{1,0:T(8,128)(2,1)S(1)}, bf16[256,768]{1,0:T(8,128)(2,1)S(1)}, u32[]{:S(2)}, u32[]{:S(2)}) %collective-permute-start.55) | collective-permute-done | bytes 393248 | tf_op jit(solution)/shard_map/ppermute | solution.py:104
  450.3 3.3 convolution_convert_fusion.3
  455.3 5.8 %add_convert_fusion.2 = bf16[1024,1536]{1,0:T(8,128)(2,1)} fusion(bf16[1024,1536]{1,0:T(8,128)(2,1)} %add_convert_fusion.3, bf16[1024,768]{1,0:T(8,128)(2,1)S(1)} %select_dynamic-update-slice_fusion.4, bf16[768,768]{1,0:T(8,128)(2,1)} %copy-done.56, bf16[768,768]{1,0:T(8,128)(2,1)S(1)} %copy-done.14), kind=kOutput, calls=%fused_computation.3 | convolution fusion | flops 2425356288 | bytes 10223616 | tf_op jit(solution)/shard_map/dot_general | solution.py:195
  470.9 3.3 convolution_convert_fusion.2
  476.3 6.6 %add_convert_fusion.1 = bf16[1024,1536]{1,0:T(8,128)(2,1)} fusion(bf16[1024,1536]{1,0:T(8,128)(2,1)} %add_convert_fusion.2, bf16[1024,768]{1,0:T(8,128)(2,1)S(1)} %select_dynamic-update-slice_fusion.3, bf16[768,768]{1,0:T(8,128)(2,1)S(1)} %copy-done.55, bf16[768,768]{1,0:T(8,128)(2,1)S(1)} %copy-done.12), kind=kOutput, calls=%fused_computation.2 | convolution fusion | flops 2425356288 | bytes 10223616 | tf_op jit(solution)/shard_map/dot_general | solution.py:195
  485.6 11.9 %collective-permute-done.59 = bf16[768,768]{1,0:T(8,128)(2,1)} collective-permute-done((bf16[768,768]{1,0:T(8,128)(2,1)S(1)}, bf16[768,768]{1,0:T(8,128)(2,1)}, u32[]{:S(2)}, u32[]{:S(2)}) %collective-permute-start.59) | collective-permute-done | bytes 1179680 | tf_op jit(solution)/shard_map/ppermute | solution.py:104
  500.5 4.6 fusion.88
  505.1 4.1 convolution_convert_fusion.1
  510.5 3.2 slice_select_fusion.2
  513.7 3.6 pad_maximum_fusion
  528.2 15.7 %collective-permute-done.61 = bf16[256,1536]{1,0:T(8,128)(2,1)S(1)} collective-permute-done((bf16[256,1536]{1,0:T(8,128)(2,1)S(1)}, bf16[256,1536]{1,0:T(8,128)(2,1)S(1)}, u32[]{:S(2)}, u32[]{:S(2)}) %collective-permute-start.61) | collective-permute-done | bytes 786464 | tf_op jit(solution)/shard_map/ppermute | solution.py:25
  (406 shorter events, 219.6 us)
Async XLA Ops:
  0.6 20.9 %collective-permute-start.1 = (bf16[256,1536]{1,0:T(8,128)(2,1)}, bf16[256,1536]{1,0:T(8,128)(2,1)}, u32[]{:S(2)}, u32[]{:S(2)}) collective-permute-start(bf16[256,1536]{1,0:T(8,128)(2,1)} %param.36), channel_id=1, source_target_pairs={{0,2},{2,0},{1,3},{3,1},{4,6},{6,4},{5,7},{7,5},{8,10},{10,8},{9,1... | collective-permute-start | bytes 2359304 | tf_op jit(solution)/shard_map/ppermute | solution.py:25
  3.6 20.7 %collective-permute-start.2 = (bf16[256,1536]{1,0:T(8,128)(2,1)}, bf16[256,1536]{1,0:T(8,128)(2,1)}, u32[]{:S(2)}, u32[]{:S(2)}) collective-permute-start(bf16[256,1536]{1,0:T(8,128)(2,1)} %param.36), channel_id=1, source_target_pairs={{0,1},{1,0},{2,3},{3,2},{4,5},{5,4},{6,7},{7,6},{8,9},{9,8},{10,11... | collective-permute-start | bytes 2359304 | tf_op jit(solution)/shard_map/ppermute | solution.py:25
  19.9 31.3 %collective-permute-start.6 = (bf16[768,768]{1,0:T(8,128)(2,1)}, bf16[768,768]{1,0:T(8,128)(2,1)}, u32[]{:S(2)}, u32[]{:S(2)}) collective-permute-start(bf16[768,768]{1,0:T(8,128)(2,1)} %get-tuple-element.341), channel_id=1, source_target_pairs={{0,1},{1,0},{2,3},{3,2},{4,5},{5,4},{6,7},{7,6},{8,9},{9,8},{10,11... | collective-permute-start | bytes 3538952 | tf_op jit(solution)/shard_map/ppermute | solution.py:25
  20.0 47.1 %collective-permute-start.8 = (bf16[768,768]{1,0:T(8,128)(2,1)}, bf16[768,768]{1,0:T(8,128)(2,1)}, u32[]{:S(2)}, u32[]{:S(2)}) collective-permute-start(bf16[768,768]{1,0:T(8,128)(2,1)} %get-tuple-element.343), channel_id=1, source_target_pairs={{0,1},{1,0},{2,3},{3,2},{4,5},{5,4},{6,7},{7,6},{8,9},{9,8},{10,11... | collective-permute-start | bytes 3538952 | tf_op jit(solution)/shard_map/ppermute | solution.py:25
  24.3 69.1 %collective-permute-start = (bf16[128,6144]{1,0:T(8,128)(2,1)}, bf16[128,6144]{1,0:T(8,128)(2,1)}, u32[]{:S(2)}, u32[]{:S(2)}) collective-permute-start(bf16[128,6144]{1,0:T(8,128)(2,1)} %broadcast_select_fusion.4), channel_id=1, source_target_pairs={{0,1},{1,0},{2,3},{3,2},{4,5},{5,4},{6,7},{7,6},{8,9},{9,8},{10,11... | collective-permute-start | bytes 4718600 | tf_op jit(solution)/shard_map/ppermute | solution.py:25
  25.9 82.4 %collective-permute-start.14 = (bf16[768,768]{1,0:T(8,128)(2,1)}, bf16[768,768]{1,0:T(8,128)(2,1)}, u32[]{:S(2)}, u32[]{:S(2)}) collective-permute-start(bf16[768,768]{1,0:T(8,128)(2,1)} %get-tuple-element.345), channel_id=1, source_target_pairs={{0,1},{1,0},{2,3},{3,2},{4,5},{5,4},{6,7},{7,6},{8,9},{9,8},{10,11... | collective-permute-start | bytes 3538952 | tf_op jit(solution)/shard_map/ppermute | solution.py:25
  36.1 29.5 %collective-permute-start.5 = (bf16[768,768]{1,0:T(8,128)(2,1)}, bf16[768,768]{1,0:T(8,128)(2,1)}, u32[]{:S(2)}, u32[]{:S(2)}) collective-permute-start(bf16[768,768]{1,0:T(8,128)(2,1)} %constant_dynamic-slice_fusion.23), channel_id=1, source_target_pairs={{0,4},{12,8},{1,5},{13,9},{2,6},{14,10},{3,7},{15,11},{16,20},{28,... | collective-permute-start | bytes 3538952 | tf_op jit(solution)/shard_map/ppermute | solution.py:77
  51.2 84.0 %collective-permute-start.22 = (bf16[768,768]{1,0:T(8,128)(2,1)}, bf16[768,768]{1,0:T(8,128)(2,1)S(1)}, u32[]{:S(2)}, u32[]{:S(2)}) collective-permute-start(bf16[768,768]{1,0:T(8,128)(2,1)} %get-tuple-element.347), channel_id=1, source_target_pairs={{0,1},{1,0},{2,3},{3,2},{4,5},{5,4},{6,7},{7,6},{8,9},{9,8},{10,11... | collective-permute-start | bytes 3538952 | tf_op jit(solution)/shard_map/ppermute | solution.py:25
  65.6 71.0 %collective-permute-start.25 = (bf16[768,768]{1,0:T(8,128)(2,1)S(1)}, bf16[768,768]{1,0:T(8,128)(2,1)S(1)}, u32[]{:S(2)}, u32[]{:S(2)}) collective-permute-start(bf16[768,768]{1,0:T(8,128)(2,1)S(1)} %copy-done.53), channel_id=1, source_target_pairs={{0,1},{1,0},{2,3},{3,2},{4,5},{5,4},{6,7},{7,6},{8,9},{9,8},{10,11... | collective-permute-start | bytes 3538952 | tf_op jit(solution)/shard_map/ppermute | solution.py:25
  71.9 47.7 %collective-permute-start.11 = (bf16[768,768]{1,0:T(8,128)(2,1)S(1)}, bf16[768,768]{1,0:T(8,128)(2,1)S(1)}, u32[]{:S(2)}, u32[]{:S(2)}) collective-permute-start(bf16[768,768]{1,0:T(8,128)(2,1)S(1)} %constant_dynamic-slice_fusion.22), channel_id=1, source_target_pairs={{0,4},{12,8},{1,5},{13,9},{2,6},{14,10},{3,7},{15,11},{16,20},{28,... | collective-permute-start | bytes 3538952 | tf_op jit(solution)/shard_map/ppermute | solution.py:77
  105.9 65.3 %collective-permute-start.32 = (bf16[768,768]{1,0:T(8,128)(2,1)S(1)}, bf16[768,768]{1,0:T(8,128)(2,1)S(1)}, u32[]{:S(2)}, u32[]{:S(2)}) collective-permute-start(bf16[768,768]{1,0:T(8,128)(2,1)S(1)} %copy-done.52), channel_id=1, source_target_pairs={{0,1},{1,0},{2,3},{3,2},{4,5},{5,4},{6,7},{7,6},{8,9},{9,8},{10,11... | collective-permute-start | bytes 3538952 | tf_op jit(solution)/shard_map/ppermute | solution.py:25
  126.8 30.8 %collective-permute-start.17 = (bf16[768,768]{1,0:T(8,128)(2,1)S(1)}, bf16[768,768]{1,0:T(8,128)(2,1)S(1)}, u32[]{:S(2)}, u32[]{:S(2)}) collective-permute-start(bf16[768,768]{1,0:T(8,128)(2,1)S(1)} %constant_dynamic-slice_fusion.21), channel_id=1, source_target_pairs={{0,4},{12,8},{1,5},{13,9},{2,6},{14,10},{3,7},{15,11},{16,20},{28,... | collective-permute-start | bytes 3538952 | tf_op jit(solution)/shard_map/ppermute | solution.py:77
  134.2 20.3 %collective-permute-start.12 = (bf16[512,768]{1,0:T(8,128)(2,1)S(1)}, bf16[512,768]{1,0:T(8,128)(2,1)S(1)}, u32[]{:S(2)}, u32[]{:S(2)}) collective-permute-start(bf16[512,768]{1,0:T(8,128)(2,1)S(1)} %constant_dynamic-slice_fusion.19), channel_id=1, source_target_pairs={{4,8},{8,4},{5,9},{9,5},{6,10},{10,6},{7,11},{11,7},{20,24},{24,20... | collective-permute-start | bytes 2359304 | tf_op jit(solution)/shard_map/ppermute | solution.py:104
  138.1 34.2 %collective-permute-start.39 = (bf16[768,768]{1,0:T(8,128)(2,1)S(1)}, bf16[768,768]{1,0:T(8,128)(2,1)S(1)}, u32[]{:S(2)}, u32[]{:S(2)}) collective-permute-start(bf16[768,768]{1,0:T(8,128)(2,1)S(1)} %copy-done.51), channel_id=1, source_target_pairs={{0,1},{1,0},{2,3},{3,2},{4,5},{5,4},{6,7},{7,6},{8,9},{9,8},{10,11... | collective-permute-start | bytes 3538952 | tf_op jit(solution)/shard_map/ppermute | solution.py:25
  158.5 39.7 %collective-permute-start.18 = (bf16[768,768]{1,0:T(8,128)(2,1)S(1)}, bf16[768,768]{1,0:T(8,128)(2,1)S(1)}, u32[]{:S(2)}, u32[]{:S(2)}) collective-permute-start(bf16[768,768]{1,0:T(8,128)(2,1)S(1)} %constant_dynamic-slice_fusion.18), channel_id=1, source_target_pairs={{0,4},{12,8},{1,5},{13,9},{2,6},{14,10},{3,7},{15,11},{16,20},{28,... | collective-permute-start | bytes 3538952 | tf_op jit(solution)/shard_map/ppermute | solution.py:77
  166.2 30.6 %collective-permute-start.20 = (bf16[512,768]{1,0:T(8,128)(2,1)S(1)}, bf16[512,768]{1,0:T(8,128)(2,1)S(1)}, u32[]{:S(2)}, u32[]{:S(2)}) collective-permute-start(bf16[512,768]{1,0:T(8,128)(2,1)S(1)} %constant_dynamic-slice_fusion.14), channel_id=1, source_target_pairs={{4,8},{8,4},{5,9},{9,5},{6,10},{10,6},{7,11},{11,7},{20,24},{24,20... | collective-permute-start | bytes 2359304 | tf_op jit(solution)/shard_map/ppermute | solution.py:104
  169.8 24.3 %collective-permute-start.23 = (bf16[256,768]{1,0:T(8,128)(2,1)S(1)}, bf16[256,768]{1,0:T(8,128)(2,1)S(1)}, u32[]{:S(2)}, u32[]{:S(2)}) collective-permute-start(bf16[256,768]{1,0:T(8,128)(2,1)S(1)} %add_convert_fusion.21), channel_id=1, source_target_pairs={{8,12},{4,0},{9,13},{5,1},{10,14},{6,2},{11,15},{7,3},{24,28},{20,... | collective-permute-start | bytes 1179656 | tf_op jit(solution)/shard_map/ppermute | solution.py:77
  174.4 44.8 %collective-permute-start.16 = (bf16[768,768]{1,0:T(8,128)(2,1)S(1)}, bf16[768,768]{1,0:T(8,128)(2,1)S(1)}, u32[]{:S(2)}, u32[]{:S(2)}) collective-permute-start(bf16[768,768]{1,0:T(8,128)(2,1)S(1)} %constant_dynamic-slice_fusion.17), channel_id=1, source_target_pairs={{8,12},{4,0},{9,13},{5,1},{10,14},{6,2},{11,15},{7,3},{24,28},{20,... | collective-permute-start | bytes 3538952 | tf_op jit(solution)/shard_map/ppermute | solution.py:104
  199.1 74.8 %collective-permute-start.27 = (bf16[768,768]{1,0:T(8,128)(2,1)}, bf16[768,768]{1,0:T(8,128)(2,1)}, u32[]{:S(2)}, u32[]{:S(2)}) collective-permute-start(bf16[768,768]{1,0:T(8,128)(2,1)} %constant_dynamic-slice_fusion.12), channel_id=1, source_target_pairs={{8,12},{4,0},{9,13},{5,1},{10,14},{6,2},{11,15},{7,3},{24,28},{20,... | collective-permute-start | bytes 3538952 | tf_op jit(solution)/shard_map/ppermute | solution.py:104
  200.4 46.3 %collective-permute-start.28 = (bf16[768,768]{1,0:T(8,128)(2,1)S(1)}, bf16[768,768]{1,0:T(8,128)(2,1)S(1)}, u32[]{:S(2)}, u32[]{:S(2)}) collective-permute-start(bf16[768,768]{1,0:T(8,128)(2,1)S(1)} %constant_dynamic-slice_fusion.13), channel_id=1, source_target_pairs={{0,4},{12,8},{1,5},{13,9},{2,6},{14,10},{3,7},{15,11},{16,20},{28,... | collective-permute-start | bytes 3538952 | tf_op jit(solution)/shard_map/ppermute | solution.py:77
  206.3 39.1 %collective-permute-start.29 = (bf16[512,768]{1,0:T(8,128)(2,1)S(1)}, bf16[512,768]{1,0:T(8,128)(2,1)S(1)}, u32[]{:S(2)}, u32[]{:S(2)}) collective-permute-start(bf16[512,768]{1,0:T(8,128)(2,1)S(1)} %constant_dynamic-slice_fusion.11), channel_id=1, source_target_pairs={{4,8},{8,4},{5,9},{9,5},{6,10},{10,6},{7,11},{11,7},{20,24},{24,20... | collective-permute-start | bytes 2359304 | tf_op jit(solution)/shard_map/ppermute | solution.py:104
  210.9 31.8 %collective-permute-start.30 = (bf16[256,768]{1,0:T(8,128)(2,1)S(1)}, bf16[256,768]{1,0:T(8,128)(2,1)S(1)}, u32[]{:S(2)}, u32[]{:S(2)}) collective-permute-start(bf16[256,768]{1,0:T(8,128)(2,1)S(1)} %add_convert_fusion.20), channel_id=1, source_target_pairs={{8,12},{4,0},{9,13},{5,1},{10,14},{6,2},{11,15},{7,3},{24,28},{20,... | collective-permute-start | bytes 1179656 | tf_op jit(solution)/shard_map/ppermute | solution.py:77
  223.4 41.8 %collective-permute-start.62 = (bf16[768,768]{1,0:T(8,128)(2,1)S(1)}, bf16[768,768]{1,0:T(8,128)(2,1)S(1)}, u32[]{:S(2)}, u32[]{:S(2)}) collective-permute-start(bf16[768,768]{1,0:T(8,128)(2,1)S(1)} %slice.749), channel_id=1, source_target_pairs={{0,1},{1,0},{2,3},{3,2},{4,5},{5,4},{6,7},{7,6},{8,9},{9,8},{10,11... | collective-permute-start | bytes 3538952 | tf_op jit(solution)/shard_map/ppermute | solution.py:25
  247.0 24.3 %collective-permute-start.31 = (bf16[512,768]{1,0:T(8,128)(2,1)S(1)}, bf16[512,768]{1,0:T(8,128)(2,1)S(1)}, u32[]{:S(2)}, u32[]{:S(2)}) collective-permute-start(bf16[512,768]{1,0:T(8,128)(2,1)S(1)} %add_convert_fusion.11), channel_id=1, source_target_pairs={{4,8},{8,4},{5,9},{9,5},{6,10},{10,6},{7,11},{11,7},{20,24},{24,20... | collective-permute-start | bytes 2359304 | tf_op jit(solution)/shard_map/ppermute | solution.py:77
  247.7 74.4 %collective-permute-start.34 = (bf16[768,768]{1,0:T(8,128)(2,1)}, bf16[768,768]{1,0:T(8,128)(2,1)}, u32[]{:S(2)}, u32[]{:S(2)}) collective-permute-start(bf16[768,768]{1,0:T(8,128)(2,1)} %constant_dynamic-slice_fusion.9), channel_id=1, source_target_pairs={{8,12},{4,0},{9,13},{5,1},{10,14},{6,2},{11,15},{7,3},{24,28},{20,... | collective-permute-start | bytes 3538952 | tf_op jit(solution)/shard_map/ppermute | solution.py:104
  254.9 40.4 %collective-permute-start.35 = (bf16[768,768]{1,0:T(8,128)(2,1)}, bf16[768,768]{1,0:T(8,128)(2,1)}, u32[]{:S(2)}, u32[]{:S(2)}) collective-permute-start(bf16[768,768]{1,0:T(8,128)(2,1)} %constant_dynamic-slice_fusion.10), channel_id=1, source_target_pairs={{0,4},{12,8},{1,5},{13,9},{2,6},{14,10},{3,7},{15,11},{16,20},{28,... | collective-permute-start | bytes 3538952 | tf_op jit(solution)/shard_map/ppermute | solution.py:77
  265.2 28.6 %collective-permute-start.36 = (bf16[512,768]{1,0:T(8,128)(2,1)}, bf16[512,768]{1,0:T(8,128)(2,1)}, u32[]{:S(2)}, u32[]{:S(2)}) collective-permute-start(bf16[512,768]{1,0:T(8,128)(2,1)} %constant_dynamic-slice_fusion.8), channel_id=1, source_target_pairs={{4,8},{8,4},{5,9},{9,5},{6,10},{10,6},{7,11},{11,7},{20,24},{24,20... | collective-permute-start | bytes 2359304 | tf_op jit(solution)/shard_map/ppermute | solution.py:104
  280.0 33.0 %collective-permute-start.63 = (bf16[768,768]{1,0:T(8,128)(2,1)}, bf16[768,768]{1,0:T(8,128)(2,1)}, u32[]{:S(2)}, u32[]{:S(2)}) collective-permute-start(bf16[768,768]{1,0:T(8,128)(2,1)} %slice.751), channel_id=1, source_target_pairs={{0,1},{1,0},{2,3},{3,2},{4,5},{5,4},{6,7},{7,6},{8,9},{9,8},{10,11... | collective-permute-start | bytes 3538952 | tf_op jit(solution)/shard_map/ppermute | solution.py:25
  296.7 21.6 %collective-permute-start.38 = (bf16[512,768]{1,0:T(8,128)(2,1)S(1)}, bf16[512,768]{1,0:T(8,128)(2,1)S(1)}, u32[]{:S(2)}, u32[]{:S(2)}) collective-permute-start(bf16[512,768]{1,0:T(8,128)(2,1)S(1)} %add_convert_fusion.10), channel_id=1, source_target_pairs={{4,8},{8,4},{5,9},{9,5},{6,10},{10,6},{7,11},{11,7},{20,24},{24,20... | collective-permute-start | bytes 2359304 | tf_op jit(solution)/shard_map/ppermute | solution.py:77
  297.5 67.5 %collective-permute-start.41 = (bf16[768,768]{1,0:T(8,128)(2,1)}, bf16[768,768]{1,0:T(8,128)(2,1)}, u32[]{:S(2)}, u32[]{:S(2)}) collective-permute-start(bf16[768,768]{1,0:T(8,128)(2,1)} %constant_dynamic-slice_fusion.6), channel_id=1, source_target_pairs={{8,12},{4,0},{9,13},{5,1},{10,14},{6,2},{11,15},{7,3},{24,28},{20,... | collective-permute-start | bytes 3538952 | tf_op jit(solution)/shard_map/ppermute | solution.py:104
  302.8 40.5 %collective-permute-start.42 = (bf16[768,768]{1,0:T(8,128)(2,1)}, bf16[768,768]{1,0:T(8,128)(2,1)}, u32[]{:S(2)}, u32[]{:S(2)}) collective-permute-start(bf16[768,768]{1,0:T(8,128)(2,1)} %constant_dynamic-slice_fusion.7), channel_id=1, source_target_pairs={{0,4},{12,8},{1,5},{13,9},{2,6},{14,10},{3,7},{15,11},{16,20},{28,... | collective-permute-start | bytes 3538952 | tf_op jit(solution)/shard_map/ppermute | solution.py:77
  313.0 28.8 %collective-permute-start.43 = (bf16[512,768]{1,0:T(8,128)(2,1)}, bf16[512,768]{1,0:T(8,128)(2,1)}, u32[]{:S(2)}, u32[]{:S(2)}) collective-permute-start(bf16[512,768]{1,0:T(8,128)(2,1)} %constant_dynamic-slice_fusion.5), channel_id=1, source_target_pairs={{4,8},{8,4},{5,9},{9,5},{6,10},{10,6},{7,11},{11,7},{20,24},{24,20... | collective-permute-start | bytes 2359304 | tf_op jit(solution)/shard_map/ppermute | solution.py:104
  328.2 29.2 %collective-permute-start.64 = (bf16[768,768]{1,0:T(8,128)(2,1)}, bf16[768,768]{1,0:T(8,128)(2,1)}, u32[]{:S(2)}, u32[]{:S(2)}) collective-permute-start(bf16[768,768]{1,0:T(8,128)(2,1)} %slice.755), channel_id=1, source_target_pairs={{0,1},{1,0},{2,3},{3,2},{4,5},{5,4},{6,7},{7,6},{8,9},{9,8},{10,11... | collective-permute-start | bytes 3538952 | tf_op jit(solution)/shard_map/ppermute | solution.py:25
  345.3 59.8 %collective-permute-start.47 = (bf16[768,768]{1,0:T(8,128)(2,1)}, bf16[768,768]{1,0:T(8,128)(2,1)}, u32[]{:S(2)}, u32[]{:S(2)}) collective-permute-start(bf16[768,768]{1,0:T(8,128)(2,1)} %constant_dynamic-slice_fusion.2), channel_id=1, source_target_pairs={{8,12},{4,0},{9,13},{5,1},{10,14},{6,2},{11,15},{7,3},{24,28},{20,... | collective-permute-start | bytes 3538952 | tf_op jit(solution)/shard_map/ppermute | solution.py:104
  350.9 40.8 %collective-permute-start.48 = (bf16[768,768]{1,0:T(8,128)(2,1)}, bf16[768,768]{1,0:T(8,128)(2,1)}, u32[]{:S(2)}, u32[]{:S(2)}) collective-permute-start(bf16[768,768]{1,0:T(8,128)(2,1)} %constant_dynamic-slice_fusion.4), channel_id=1, source_target_pairs={{0,4},{12,8},{1,5},{13,9},{2,6},{14,10},{3,7},{15,11},{16,20},{28,... | collective-permute-start | bytes 3538952 | tf_op jit(solution)/shard_map/ppermute | solution.py:77
  357.4 31.7 %collective-permute-start.49 = (bf16[512,768]{1,0:T(8,128)(2,1)}, bf16[512,768]{1,0:T(8,128)(2,1)}, u32[]{:S(2)}, u32[]{:S(2)}) collective-permute-start(bf16[512,768]{1,0:T(8,128)(2,1)} %constant_dynamic-slice_fusion.1), channel_id=1, source_target_pairs={{4,8},{8,4},{5,9},{9,5},{6,10},{10,6},{7,11},{11,7},{20,24},{24,20... | collective-permute-start | bytes 2359304 | tf_op jit(solution)/shard_map/ppermute | solution.py:104
  363.5 21.5 %collective-permute-start.50 = (bf16[256,768]{1,0:T(8,128)(2,1)}, bf16[256,768]{1,0:T(8,128)(2,1)}, u32[]{:S(2)}, u32[]{:S(2)}) collective-permute-start(bf16[256,768]{1,0:T(8,128)(2,1)} %add_convert_fusion.17), channel_id=1, source_target_pairs={{8,12},{4,0},{9,13},{5,1},{10,14},{6,2},{11,15},{7,3},{24,28},{20,... | collective-permute-start | bytes 1179656 | tf_op jit(solution)/shard_map/ppermute | solution.py:77
  371.2 28.7 %collective-permute-start.65 = (bf16[768,768]{1,0:T(8,128)(2,1)}, bf16[768,768]{1,0:T(8,128)(2,1)}, u32[]{:S(2)}, u32[]{:S(2)}) collective-permute-start(bf16[768,768]{1,0:T(8,128)(2,1)} %slice.759), channel_id=1, source_target_pairs={{0,1},{1,0},{2,3},{3,2},{4,5},{5,4},{6,7},{7,6},{8,9},{9,8},{10,11... | collective-permute-start | bytes 3538952 | tf_op jit(solution)/shard_map/ppermute | solution.py:25
  390.4 58.2 %collective-permute-start.53 = (bf16[768,768]{1,0:T(8,128)(2,1)}, bf16[768,768]{1,0:T(8,128)(2,1)}, u32[]{:S(2)}, u32[]{:S(2)}) collective-permute-start(bf16[768,768]{1,0:T(8,128)(2,1)} %constant_dynamic-slice_fusion), channel_id=1, source_target_pairs={{8,12},{4,0},{9,13},{5,1},{10,14},{6,2},{11,15},{7,3},{24,28},{20,... | collective-permute-start | bytes 3538952 | tf_op jit(solution)/shard_map/ppermute | solution.py:104
  398.3 39.8 %collective-permute-start.56 = (bf16[512,768]{1,0:T(8,128)(2,1)}, bf16[512,768]{1,0:T(8,128)(2,1)}, u32[]{:S(2)}, u32[]{:S(2)}) collective-permute-start(bf16[512,768]{1,0:T(8,128)(2,1)} %constant_dynamic-slice_fusion.16), channel_id=1, source_target_pairs={{4,8},{8,4},{5,9},{9,5},{6,10},{10,6},{7,11},{11,7},{20,24},{24,20... | collective-permute-start | bytes 2359304 | tf_op jit(solution)/shard_map/ppermute | solution.py:104
  403.5 25.0 %collective-permute-start.54 = (bf16[256,768]{1,0:T(8,128)(2,1)S(1)}, bf16[256,768]{1,0:T(8,128)(2,1)}, u32[]{:S(2)}, u32[]{:S(2)}) collective-permute-start(bf16[256,768]{1,0:T(8,128)(2,1)S(1)} %add_convert_fusion.16), channel_id=1, source_target_pairs={{8,12},{4,0},{9,13},{5,1},{10,14},{6,2},{11,15},{7,3},{24,28},{20,... | collective-permute-start | bytes 1179656 | tf_op jit(solution)/shard_map/ppermute | solution.py:77
  411.2 49.9 %collective-permute-start.66 = (bf16[768,768]{1,0:T(8,128)(2,1)}, bf16[768,768]{1,0:T(8,128)(2,1)}, u32[]{:S(2)}, u32[]{:S(2)}) collective-permute-start(bf16[768,768]{1,0:T(8,128)(2,1)} %slice.763), channel_id=1, source_target_pairs={{0,1},{1,0},{2,3},{3,2},{4,5},{5,4},{6,7},{7,6},{8,9},{9,8},{10,11... | collective-permute-start | bytes 3538952 | tf_op jit(solution)/shard_map/ppermute | solution.py:25
  439.5 29.7 %collective-permute-start.57 = (bf16[768,768]{1,0:T(8,128)(2,1)}, bf16[768,768]{1,0:T(8,128)(2,1)}, u32[]{:S(2)}, u32[]{:S(2)}) collective-permute-start(bf16[768,768]{1,0:T(8,128)(2,1)} %constant_dynamic-slice_fusion.3), channel_id=1, source_target_pairs={{8,12},{4,0},{9,13},{5,1},{10,14},{6,2},{11,15},{7,3},{24,28},{20,... | collective-permute-start | bytes 3538952 | tf_op jit(solution)/shard_map/ppermute | solution.py:104
  454.8 28.1 %collective-permute-start.67 = (bf16[768,768]{1,0:T(8,128)(2,1)}, bf16[768,768]{1,0:T(8,128)(2,1)S(1)}, u32[]{:S(2)}, u32[]{:S(2)}) collective-permute-start(bf16[768,768]{1,0:T(8,128)(2,1)} %slice.767), channel_id=1, source_target_pairs={{0,1},{1,0},{2,3},{3,2},{4,5},{5,4},{6,7},{7,6},{8,9},{9,8},{10,11... | collective-permute-start | bytes 3538952 | tf_op jit(solution)/shard_map/ppermute | solution.py:25
  465.0 32.4 %collective-permute-start.59 = (bf16[768,768]{1,0:T(8,128)(2,1)S(1)}, bf16[768,768]{1,0:T(8,128)(2,1)}, u32[]{:S(2)}, u32[]{:S(2)}) collective-permute-start(bf16[768,768]{1,0:T(8,128)(2,1)S(1)} %constant_dynamic-slice_fusion.15), channel_id=1, source_target_pairs={{8,12},{4,0},{9,13},{5,1},{10,14},{6,2},{11,15},{7,3},{24,28},{20,... | collective-permute-start | bytes 3538952 | tf_op jit(solution)/shard_map/ppermute | solution.py:104
  475.3 42.8 %collective-permute-start.68 = (bf16[768,768]{1,0:T(8,128)(2,1)}, bf16[768,768]{1,0:T(8,128)(2,1)}, u32[]{:S(2)}, u32[]{:S(2)}) collective-permute-start(bf16[768,768]{1,0:T(8,128)(2,1)} %slice.771), channel_id=1, source_target_pairs={{0,1},{1,0},{2,3},{3,2},{4,5},{5,4},{6,7},{7,6},{8,9},{9,8},{10,11... | collective-permute-start | bytes 3538952 | tf_op jit(solution)/shard_map/ppermute | solution.py:25
  499.6 23.7 %collective-permute-start.70 = (f32[6144]{0:T(1024)S(1)}, f32[6144]{0:T(1024)S(1)}, u32[]{:S(2)}, u32[]{:S(2)}) collective-permute-start(f32[6144]{0:T(1024)S(1)} %constant_dynamic-update-slice_fusion.8), channel_id=1, source_target_pairs={{0,1},{1,0},{2,3},{3,2},{4,5},{5,4},{6,7},{7,6},{8,9},{9,8},{10,11... | collective-permute-start | bytes 73736 | tf_op jit(solution)/shard_map/ppermute | solution.py:25
  523.9 20.0 %collective-permute-start.61 = (bf16[256,1536]{1,0:T(8,128)(2,1)S(1)}, bf16[256,1536]{1,0:T(8,128)(2,1)S(1)}, u32[]{:S(2)}, u32[]{:S(2)}) collective-permute-start(bf16[256,1536]{1,0:T(8,128)(2,1)S(1)} %select_convert_fusion.1), channel_id=1, source_target_pairs={{0,2},{2,0},{1,3},{3,1},{4,6},{6,4},{5,7},{7,5},{8,10},{10,8},{9,1... | collective-permute-start | bytes 2359304 | tf_op jit(solution)/shard_map/ppermute | solution.py:25
  (85 other events, 769.6 us)
